TPU v7x, 768 devices: a whole 4x8x12 slice. The times are simulated.
768 devices in a mesh: seq: 96 (over x, z, core), grp: 8 (over y).
Axes of the slice: x: 4, y: 8, z: 12, core: 2. Of those that a mesh axis runs over, the one named last changes fastest.
Arguments:
- queries: bfloat16 [8, 12288, 1024], P('grp', 'seq'), may hold values from -6 to 6
- key_rows: bfloat16 [8, 12288, 1024], P('grp', 'seq'), may hold values from -6 to 6
- value_rows: bfloat16 [8, 12288, 1024], P('grp', 'seq'), may hold values from -6 to 6
- out_grad: bfloat16 [8, 12288, 1024], P('grp', 'seq'), may hold values from -6 to 6
- positions: int32 [8, 96], P('grp', 'seq'), may hold values from 0 to 2, as said below
- user_len: int32 [8, 96], P('grp', 'seq'), may hold values from 1 to 384, as said below
- position_bias: float32 [8, 384], replicated, may hold values from -3 to 3
Outputs:
- attended: bfloat16 [8, 12288, 1024], P('grp', 'seq')
- query_grad: bfloat16 [8, 12288, 1024], P('grp', 'seq')
- key_grad: bfloat16 [8, 12288, 1024], P('grp', 'seq')
- value_grad: bfloat16 [8, 12288, 1024], P('grp', 'seq')
- bias_grad: float32 [8, 384], replicated
Inputs may be any that keep to these rules, and one draw needn't show every extreme that they name: `positions`: along seq within one grp index, histories occupy consecutive blocks numbered 0, 1, ... from the first; the first history of every group has exactly 3 blocks; no history has more than 3 blocks. `user_len`: equal on all blocks of one history; a history of b blocks has between (b - 1) * 128 + 1 and b * 128 events, so all its blocks but the last are full.
All inputs are finite; a program needn't handle non-finite values.
Results may differ from a plain program's by a relative error of at most 0.0053.
Values may be sent and summed in bfloat16 or wider, within the bound.
A program may use at most 32 MiB of HBM per device.

v0:
```python
import jax
import jax.numpy as jnp
from jax import lax
from jax.sharding import PartitionSpec as P

H = 8
SPAN = 3


def passed_along(block, axis, distance):
    devices = range(lax.axis_size(axis))
    route = [(i - distance, i) for i in devices if i - distance in devices]
    return lax.ppermute(block, axis, route)


def settle(values):
    return lax.optimization_barrier(values.astype(jnp.bfloat16)).astype(jnp.float32)


def toeplitz(bias_table, offset, block_rows):
    padded = jnp.pad(bias_table, ((0, 0), (block_rows, 0)))
    first_col = offset * block_rows + 1
    window = padded[:, first_col : first_col + 2 * block_rows - 1]
    flipped = window[:, ::-1]
    extended = jnp.concatenate([flipped, jnp.zeros_like(flipped[:, :1])], axis=1)
    rolled = jnp.roll(extended, -(block_rows - 1), axis=1)
    tiling = jnp.tile(rolled, (1, block_rows))[:, : block_rows * (2 * block_rows - 1)]
    return tiling.reshape(bias_table.shape[0], block_rows, 2 * block_rows - 1)[:, :, :block_rows]


def pair_terms(
    query_blk, key_blk, value_blk, grad_blk, offset, rows_valid, length, position_bias, active
):
    block_rows, width = query_blk.shape
    head_dim = width // H
    score_scale = head_dim ** (-0.5)

    def compute(unused):
        row_index = jnp.arange(block_rows, dtype=jnp.int32)
        distance = offset * block_rows + row_index[:, None] - row_index[None, :]
        usable = ((distance >= 0) & (row_index[:, None] < rows_valid))[None]
        near, near_back = jax.vjp(
            lambda bias_table: toeplitz(bias_table, offset, block_rows), position_bias
        )
        query_heads = query_blk.reshape(block_rows, H, head_dim)
        key_heads = key_blk.reshape(block_rows, H, head_dim)
        value_heads = value_blk.reshape(block_rows, H, head_dim)
        grad_heads = grad_blk.reshape(block_rows, H, head_dim)
        scores = (
            jnp.einsum("rhd,chd->hrc", query_heads, key_heads, preferred_element_type=jnp.float32)
            * score_scale
            + near
        )
        sigmoid_part = jax.nn.sigmoid(scores)
        inverse = 1.0 / jnp.maximum(length, 1).astype(jnp.float32)
        weights = jnp.where(usable, scores * sigmoid_part * inverse, 0.0).astype(jnp.bfloat16)
        attended = jnp.einsum(
            "hrc,chd->rhd", weights, value_heads, preferred_element_type=jnp.float32
        ).reshape(block_rows, width)
        pulled = jnp.einsum(
            "rhd,chd->hrc", grad_heads, value_heads, preferred_element_type=jnp.float32
        )
        slopes = jnp.where(
            usable, pulled * sigmoid_part * (1.0 + scores * (1.0 - sigmoid_part)) * inverse, 0.0
        )
        slopes_low = slopes.astype(jnp.bfloat16)
        query_grad = (
            jnp.einsum(
                "hrc,chd->rhd", slopes_low, key_heads, preferred_element_type=jnp.float32
            ).reshape(block_rows, width)
            * score_scale
        )
        key_grad = (
            jnp.einsum(
                "hrc,rhd->chd", slopes_low, query_heads, preferred_element_type=jnp.float32
            ).reshape(block_rows, width)
            * score_scale
        )
        value_grad = jnp.einsum(
            "hrc,rhd->chd", weights, grad_heads, preferred_element_type=jnp.float32
        ).reshape(block_rows, width)
        bias_part = near_back(slopes)[0]
        return (attended, query_grad, key_grad, value_grad, bias_part)

    def skipped(unused):
        empty = jnp.zeros((block_rows, width), jnp.float32)
        return (empty, empty, empty, empty, jnp.zeros(position_bias.shape, jnp.float32))

    return lax.cond(active, compute, skipped, None)


def on_device(queries, key_rows, value_rows, out_grad, positions, user_len, position_bias):
    query_blk = queries[0]
    key_blk = key_rows[0]
    value_blk = value_rows[0]
    grad_blk = out_grad[0]
    block_rows = query_blk.shape[0]
    place = positions[0, 0]
    length = user_len[0, 0]
    rows_valid = jnp.clip(length - place * block_rows, 0, block_rows)
    totals = list(
        pair_terms(
            query_blk,
            key_blk,
            value_blk,
            grad_blk,
            0,
            rows_valid,
            length,
            position_bias,
            jnp.asarray(True),
        )
    )
    for offset in range(1, SPAN):
        moved = passed_along((key_blk, value_blk), "seq", offset)
        terms = pair_terms(
            query_blk,
            moved[0],
            moved[1],
            grad_blk,
            offset,
            rows_valid,
            length,
            position_bias,
            place >= offset,
        )
        returned = passed_along(
            (terms[2].astype(jnp.bfloat16), terms[3].astype(jnp.bfloat16)), "seq", -offset
        )
        totals = [
            totals[0] + settle(terms[0]),
            totals[1] + settle(terms[1]),
            totals[2] + returned[0].astype(jnp.float32),
            totals[3] + returned[1].astype(jnp.float32),
            totals[4] + terms[4],
        ]
    summed = lax.psum(totals[4], ("seq", "grp"))
    bias_grad = summed * (lax.axis_size("seq") * lax.axis_size("grp")) ** (-0.5)
    return (
        totals[0].astype(jnp.bfloat16)[None],
        totals[1].astype(jnp.bfloat16)[None],
        totals[2].astype(jnp.bfloat16)[None],
        totals[3].astype(jnp.bfloat16)[None],
        bias_grad,
    )


def solution(mesh):
    return jax.shard_map(
        on_device,
        mesh=mesh,
        in_specs=(
            P("grp", "seq", None),
            P("grp", "seq", None),
            P("grp", "seq", None),
            P("grp", "seq", None),
            P("grp", "seq"),
            P("grp", "seq"),
            P(),
        ),
        out_specs=(
            P("grp", "seq", None),
            P("grp", "seq", None),
            P("grp", "seq", None),
            P("grp", "seq", None),
            P(),
        ),
        check_vma=False,
    )
```

profile of v0, /device:TPU:1, one launch (start us, length us, event | category | flops | bytes accessed | tf_op | source)
XLA Modules:
  0.0 192.7 jit_solution(13227728786345411435)
XLA Ops:
  0.6 1.1 copy.107
  1.8 5.5 %collective-permute-start.2 = (bf16[128,1024]{0,1:T(8,128)(2,1)S(1)}, bf16[128,1024]{0,1:T(8,128)(2,1)}, u32[]{:S(2)}, u32[]{:S(2)}) collective-permute-start(bf16[128,1024]{0,1:T(8,128)(2,1)S(1)} %bitcast.135), channel_id=1, source_target_pairs={{0,16},{8,24},{16,32},{24,40},{32,48},{40,56},{48,64},{56,72},{64,... | collective-permute-start | bytes 786440 | tf_op jit(solution)/shard_map/ppermute | solution.py:13
  7.3 4.2 %collective-permute-start = (bf16[128,1024]{0,1:T(8,128)(2,1)S(1)}, bf16[128,1024]{0,1:T(8,128)(2,1)}, u32[]{:S(2)}, u32[]{:S(2)}) collective-permute-start(bf16[128,1024]{0,1:T(8,128)(2,1)S(1)} %bitcast.136), channel_id=1, source_target_pairs={{0,8},{8,16},{16,24},{24,32},{32,40},{40,48},{48,56},{56,64},{64,7... | collective-permute-start | bytes 786440 | tf_op jit(solution)/shard_map/ppermute | solution.py:13
  11.5 4.7 %collective-permute-start.3 = (bf16[128,1024]{1,0:T(8,128)(2,1)}, bf16[128,1024]{1,0:T(8,128)(2,1)}, u32[]{:S(2)}, u32[]{:S(2)}) collective-permute-start(bf16[128,1024]{1,0:T(8,128)(2,1)} %bitcast.33), channel_id=1, source_target_pairs={{0,16},{8,24},{16,32},{24,40},{32,48},{40,56},{48,64},{56,72},{64,... | collective-permute-start | bytes 786440 | tf_op jit(solution)/shard_map/ppermute | solution.py:13
  16.2 1.9 collective-permute-start.1
  19.6 0.1 reverse.7
  19.9 0.1 fusion.47
  20.0 1.7 copy.111
  21.8 0.2 copy.106
  22.0 0.8 copy-done.1
  22.7 0.2 copy.108
  23.1 1.4 reshape.227
  24.6 0.3 fusion.35
  24.9 0.7 copy-done.10
  25.6 0.3 fusion.42
  25.9 0.4 fusion.34
  26.3 0.3 fusion.50
  26.6 1.0 copy.90
  27.6 1.0 copy.76
  28.6 0.3 fusion.30
  29.0 1.0 copy.87
  30.0 0.3 fusion.31
  30.3 1.0 copy.84
  31.3 0.1 pad.70
  31.4 0.6 reshape.230
  32.1 0.1 reduce_sum.27
  32.4 0.1 reverse.8
  32.6 14.0 %conditional.2 = (bf16[128,1024]{0,1:T(8,128)(2,1)}, bf16[128,1024]{0,1:T(8,128)(2,1)}, bf16[128,1024]{0,1:T(8,128)(2,1)}, bf16[128,1024]{0,1:T(8,128)(2,1)S(1)}, f32[8,384]{1,0:T(8,128)S(1)}) conditional(s32[]{:T(128)} %bitcast.31, () %tuple.24, (s32[]{:T(128)}, bf16[1,128,1024]{2,1,0:T(8,128)(2,1)S(1)}, bf16[128,1024]{0,1:T(8,128)(2,1)}, ...), branch_computations={%region_0.1_spmd, %region_1.3_spmd} | conditional | flops 205834496 | bytes 22766528 | solution.py:89
  33.5 0.1 reverse.3
  33.9 0.1 fusion.13
  34.0 0.2 copy.74
  34.2 0.2 copy.73
  34.5 1.4 reshape.209
  35.9 1.2 fusion.5
  37.2 1.0 fusion.14
  38.2 1.3 fusion.4
  39.5 2.0 %fusion.6 = bf16[8,128,128]{1,2,0:T(8,128)(2,1)} fusion(f32[8,128,128]{2,1,0:T(8,128)S(1)} %fusion.5, f32[]{:T(128)S(6)} %div.13, pred[128,128]{1,0:T(8,128)(4,1)S(1)} %fusion.13, bf16[128,1024]{1,0:T(8,128)(2,1)} %get-tuple-element.33), kind=kOutput, calls=%fused_computation.12 | convolution fusion | flops 34471936 | bytes 1064964 | tf_op jit(solution)/shard_map/cond/branch_1_fun/hrc,chd->rhd/dot_general | solution.py:57
  41.5 0.3 fusion
  41.9 0.9 copy.59
  42.7 1.3 fusion.1
  44.0 0.9 copy.57
  44.8 0.1 pad.50
  44.9 0.6 reshape.213
  45.6 0.1 reduce_sum.24
  45.9 0.1 reverse.4
  46.2 0.3 copy-done.8
  46.6 1.8 copy.75
  48.4 0.9 copy.89
  49.2 1.9 collective-permute-start.6
  51.1 1.9 collective-permute-start.4
  53.1 0.3 conditional.3
  53.4 0.1 copy.79
  53.6 0.1 copy.91
  53.7 1.3 collective-permute-start.7
  55.1 1.4 collective-permute-start.5
  56.5 0.8 fusion.40
  57.3 0.1 fusion.39
  57.5 129.9 %psum.7 = f32[8,384]{1,0:T(8,128)S(1)} all-reduce(f32[8,384]{1,0:T(8,128)S(1)} %fusion.49), channel_id=1, replica_groups=mesh['seq'=96,'grp'=8] {'seq','grp'}, use_global_device_ids=true, to_apply=%region_7.8 | all-reduce | flops 3072 | bytes 24576 | tf_op jit(solution)/shard_map/psum | solution.py:137
  187.4 0.6 broadcast_multiply_fusion
  188.0 0.8 copy.92
  188.9 1.1 fusion.37
  190.0 0.9 copy.93
  190.8 0.2 copy-done.2
  191.0 1.7 fusion.41
  (60 shorter events, 2.1 us)
Async XLA Ops:
  0.6 17.5 %copy-start.12 = (f32[8,384]{1,0:T(8,128)S(1)}, f32[8,384]{1,0:T(8,128)}, u32[]{:S(2)}) copy-start(f32[8,384]{1,0:T(8,128)} %param.17) | copy-start | bytes 36868
  1.8 51.3 %collective-permute-start.2 = (bf16[128,1024]{0,1:T(8,128)(2,1)S(1)}, bf16[128,1024]{0,1:T(8,128)(2,1)}, u32[]{:S(2)}, u32[]{:S(2)}) collective-permute-start(bf16[128,1024]{0,1:T(8,128)(2,1)S(1)} %bitcast.135), channel_id=1, source_target_pairs={{0,16},{8,24},{16,32},{24,40},{32,48},{40,56},{48,64},{56,72},{64,... | collective-permute-start | bytes 786440 | tf_op jit(solution)/shard_map/ppermute | solution.py:13
  7.3 25.3 %collective-permute-start = (bf16[128,1024]{0,1:T(8,128)(2,1)S(1)}, bf16[128,1024]{0,1:T(8,128)(2,1)}, u32[]{:S(2)}, u32[]{:S(2)}) collective-permute-start(bf16[128,1024]{0,1:T(8,128)(2,1)S(1)} %bitcast.136), channel_id=1, source_target_pairs={{0,8},{8,16},{16,24},{24,32},{32,40},{40,48},{48,56},{56,64},{64,7... | collective-permute-start | bytes 786440 | tf_op jit(solution)/shard_map/ppermute | solution.py:13
  11.5 41.6 %collective-permute-start.3 = (bf16[128,1024]{1,0:T(8,128)(2,1)}, bf16[128,1024]{1,0:T(8,128)(2,1)}, u32[]{:S(2)}, u32[]{:S(2)}) collective-permute-start(bf16[128,1024]{1,0:T(8,128)(2,1)} %bitcast.33), channel_id=1, source_target_pairs={{0,16},{8,24},{16,32},{24,40},{32,48},{40,56},{48,64},{56,72},{64,... | collective-permute-start | bytes 786440 | tf_op jit(solution)/shard_map/ppermute | solution.py:13
  16.2 16.4 %collective-permute-start.1 = (bf16[128,1024]{1,0:T(8,128)(2,1)}, bf16[128,1024]{1,0:T(8,128)(2,1)}, u32[]{:S(2)}, u32[]{:S(2)}) collective-permute-start(bf16[128,1024]{1,0:T(8,128)(2,1)} %bitcast.33), channel_id=1, source_target_pairs={{0,8},{8,16},{16,24},{24,32},{32,40},{40,48},{48,56},{56,64},{64,7... | collective-permute-start | bytes 786440 | tf_op jit(solution)/shard_map/ppermute | solution.py:13
  20.0 1.8 copy-start
  21.8 1.0 copy-start.1
  24.6 1.0 copy-start.10
  45.6 1.0 copy-start.8
  49.2 141.6 %collective-permute-start.6 = (bf16[128,1024]{1,0:T(8,128)(2,1)}, bf16[128,1024]{1,0:T(8,128)(2,1)}, u32[]{:S(2)}, u32[]{:S(2)}) collective-permute-start(bf16[128,1024]{1,0:T(8,128)(2,1)} %copy.89), channel_id=1, source_target_pairs={{8,0},{16,8},{24,16},{32,24},{40,32},{48,40},{56,48},{64,56},{72,6... | collective-permute-start | bytes 786440 | tf_op jit(solution)/shard_map/ppermute | solution.py:13
  51.1 137.7 %collective-permute-start.4 = (bf16[128,1024]{0,1:T(8,128)(2,1)}, bf16[128,1024]{0,1:T(8,128)(2,1)}, u32[]{:S(2)}, u32[]{:S(2)}) collective-permute-start(bf16[128,1024]{0,1:T(8,128)(2,1)} %get-tuple-element.61), channel_id=1, source_target_pairs={{8,0},{16,8},{24,16},{32,24},{40,32},{48,40},{56,48},{64,56},{72,6... | collective-permute-start | bytes 786440 | tf_op jit(solution)/shard_map/ppermute | solution.py:13
  53.4 3.1 %copy-start.4 = (f32[128,1024]{1,0:T(8,128)S(1)}, f32[128,1024]{1,0:T(8,128)}, u32[]{:S(2)}) copy-start(f32[128,1024]{1,0:T(8,128)} %copy.76) | copy-start | bytes 1572868
  53.6 2.9 %copy-start.6 = (bf16[128,1024]{1,0:T(8,128)(2,1)S(1)}, bf16[128,1024]{1,0:T(8,128)(2,1)}, u32[]{:S(2)}) copy-start(bf16[128,1024]{1,0:T(8,128)(2,1)} %copy.75) | copy-start | bytes 786436
  53.7 137.1 %collective-permute-start.7 = (bf16[128,1024]{1,0:T(8,128)(2,1)S(1)}, bf16[128,1024]{1,0:T(8,128)(2,1)S(1)}, u32[]{:S(2)}, u32[]{:S(2)}) collective-permute-start(bf16[128,1024]{1,0:T(8,128)(2,1)S(1)} %copy.91), channel_id=1, source_target_pairs={{16,0},{24,8},{32,16},{40,24},{48,32},{56,40},{64,48},{72,56},{80,... | collective-permute-start | bytes 786440 | tf_op jit(solution)/shard_map/ppermute | solution.py:13
  55.0 2.3 %copy-start.5 = (f32[128,8,128]{0,2,1:T(8,128)S(1)}, f32[128,8,128]{0,2,1:T(8,128)}, u32[]{:S(2)}) copy-start(f32[128,8,128]{0,2,1:T(8,128)} %copy.84) | copy-start | bytes 1572868
  55.0 2.3 %copy-start.7 = (bf16[128,1024]{0,1:T(8,128)(2,1)S(1)}, bf16[128,1024]{0,1:T(8,128)(2,1)}, u32[]{:S(2)}) copy-start(bf16[128,1024]{0,1:T(8,128)(2,1)} %get-tuple-element.59) | copy-start | bytes 786436
  55.1 133.8 %collective-permute-start.5 = (bf16[128,1024]{0,1:T(8,128)(2,1)S(1)}, bf16[128,1024]{0,1:T(8,128)(2,1)S(1)}, u32[]{:S(2)}, u32[]{:S(2)}) collective-permute-start(bf16[128,1024]{0,1:T(8,128)(2,1)S(1)} %get-tuple-element.62), channel_id=1, source_target_pairs={{16,0},{24,8},{32,16},{40,24},{48,32},{56,40},{64,48},{72,56},{80,... | collective-permute-start | bytes 786440 | tf_op jit(solution)/shard_map/ppermute | solution.py:13
  57.4 131.4 %copy-start.3 = (f32[128,8,128]{0,2,1:T(8,128)S(1)}, f32[128,8,128]{0,2,1:T(8,128)}, u32[]{:S(2)}) copy-start(f32[128,8,128]{0,2,1:T(8,128)} %copy.87) | copy-start | bytes 1572868
  189.9 1.0 copy-start.2
where the time goes:
time: 194 us; the launch traced here: 193 us
  blocking collectives  130 us (67%)
  starting transfers between devices  22.8 us (12%)
  local copies, waits for them, and re-layouts  22.3 us (11%)
  matrix products  9.12 us (5%)
  other arithmetic  5.2 us (3%)
  between operations  2.32 us (1%)
    psum x1, blocking collectives, on_device(): summed = lax.psum(totals[4], ('seq', 'grp'))  130 us
    ppermute x8, starting transfers between devices, passed_along(): return lax.ppermute(block, axis, route)  22.8 us
    unnamed x27, local copies, waits for them, and re-layouts  5.54 us
    reshape x4, local copies, waits for them, and re-layouts, toeplitz(): tiling.reshape(bias_table.shape[0], block_rows, 2 * block_rows - 1)  4.02 us
  transfers between devices with their start and end apart: 8, of which 0 were waited for; matrix products, arithmetic and copies ran while one was open for 16% of the time, Pallas kernels for 0%

commit v1 on v0

v1 whole, which is shorter than its diff:
```python
import jax
import jax.numpy as jnp
from jax import lax
from jax.experimental import pallas as pl
from jax.experimental.pallas import tpu as pltpu
from jax.sharding import PartitionSpec as P

H = 8
BLOCK = 128
D = 1024
MESH = pl.DeviceIdType.MESH
F32 = jnp.float32
BF16 = jnp.bfloat16
SCALE = 128 ** -0.5


def own_row(side):
    return pl.multiple_of(256 * (1 - side), 128)


def far_row(side):
    return pl.multiple_of(256 * side, 128)


def head_cols(h):
    return pl.ds(pl.multiple_of(h * 128, 128), 128)


def flip(x):
    lane = lax.broadcasted_iota(jnp.int32, x.shape, 1)
    return jnp.take_along_axis(x, 127 - lane, axis=1, mode="promise_in_bounds")


def skew(x, left):
    width = x.shape[1]
    row = lax.broadcasted_iota(jnp.int32, x.shape, 0)
    for bit in (1, 2, 4):
        moved = pltpu.roll(x, width - bit if left else bit, 1)
        x = jnp.where((row & bit) != 0, moved, x)
    return x


def nt(a, b):
    return lax.dot_general(a, b, (((1,), (1,)), ((), ())), preferred_element_type=F32)


def diagonals(slopes, width):
    total = None
    for i in range(16):
        slab = slopes[8 * i : 8 * i + 8]
        if i:
            slab = pltpu.roll(slab, width - 8 * i, 1)
        total = slab if total is None else total + slab
    return skew(total, True)


def main_kernel(
    q_ref, k_ref, v_ref, g_ref, pos_ref, len_ref, bias_ref,
    res_ref, bg_ref,
    wide, toep, mask, outb, acc, bl, r1, r2, fin,
    load_sem, chip_send, chip_recv, w1_send, w1_recv, rel_send, rel_recv, w2_send, w2_recv,
    ar_send, ar_recv, out_sem,
):
    s = lax.axis_index("seq")
    grp = lax.axis_index("grp")
    n_seq = lax.axis_size("seq")
    n_grp = lax.axis_size("grp")
    c = s % 2
    x = s // 24
    m = s % 24
    d = 1 - c
    e = c
    sib = {"seq": s + 1 - 2 * c, "grp": grp}
    ahead = {"seq": (s + 4 * c - 2 + n_seq) % n_seq, "grp": grp}
    behind = {"seq": (s + 2 - 4 * c + n_seq) % n_seq, "grp": grp}

    loads = []
    for i, (ref, side, part) in enumerate(
        ((q_ref, 1, 0), (g_ref, 1, 1), (k_ref, 0, 0), (v_ref, 0, 1))
    ):
        row = 256 * (1 - side)
        copy = pltpu.make_async_copy(
            ref.at[0], wide.at[side, part, pl.ds(row, 128)], load_sem.at[i]
        )
        copy.start()
        loads.append(copy)

    barrier = pltpu.get_barrier_semaphore()

    def greet(device):
        pl.semaphore_signal(barrier, inc=1, device_id=device, device_id_type=MESH)

    def line_peer(j):
        return {"seq": x * 24 + (m + j) % 24, "grp": grp}

    def plane_peer(j):
        t = (x * n_grp + grp + j) % 32
        return {"seq": (t // n_grp) * 24 + m, "grp": t % n_grp}

    greet(ahead)
    greet(behind)

    def greet_line(j, carry):
        greet(line_peer(j))
        return carry

    def greet_plane(j, carry):
        greet(plane_peer(j))
        return carry

    lax.fori_loop(1, 24, greet_line, 0)
    lax.fori_loop(1, 32, greet_plane, 0)

    p = pos_ref[0, 0]
    n = len_ref[0, 0]
    row = lax.broadcasted_iota(jnp.int32, (128, 384), 0)
    lane = lax.broadcasted_iota(jnp.int32, (128, 384), 1)
    inverse = 1.0 / jnp.full((128, 384), n, jnp.int32).astype(F32)
    used = (row < n - p * 128) & (lane >= 256 - 128 * p) & (lane <= 256 + row)
    mask[0] = jnp.where(used, inverse, 0.0)
    used = (lane < n - p * 128) & (lane >= row)
    mask[1] = jnp.where(used, inverse, 0.0)

    def make_toep(h, carry):
        b = jnp.broadcast_to(bias_ref[pl.ds(h, 1), :] * 0.5, (8, 384))
        b0, b1, b2 = b[:, :128], b[:, 128:256], b[:, 256:]
        zero = jnp.zeros_like(b0)
        keyed = skew(jnp.concatenate([b0, b1, b2, zero], axis=1), False)
        quer = jnp.concatenate([flip(b1), flip(b0), zero, flip(b2)], axis=1)
        quer = skew(pltpu.roll(quer, 1, 1), False)
        for i in range(16):
            toep[1, h, 8 * i : 8 * i + 8, :] = (pltpu.roll(keyed, 8 * i, 1) if i else keyed)[:, :384]
            toep[0, h, 8 * i : 8 * i + 8, :] = (pltpu.roll(quer, 8 * i, 1) if i else quer)[:, :384]
        return carry

    lax.fori_loop(0, H, make_toep, 0)

    for copy in loads:
        copy.wait()
    pl.semaphore_wait(barrier, 2 + 23 + 31)

    def piece(side, part, rows, h):
        return wide.at[side, part, pl.ds(rows, 128), head_cols(h)]

    def first_copy(h, part):
        return pltpu.make_async_remote_copy(
            src_ref=piece(d, part, own_row(d), h), dst_ref=piece(d, part, far_row(d), h),
            send_sem=w1_send.at[h, part], recv_sem=w1_recv.at[h, part],
            device_id=ahead, device_id_type=MESH,
        )

    def second_copy(h, part):
        return pltpu.make_async_remote_copy(
            src_ref=piece(e, part, own_row(e), h), dst_ref=piece(e, part, far_row(e), h),
            send_sem=w2_send.at[h, part], recv_sem=w2_recv.at[h, part],
            device_id=behind, device_id_type=MESH,
        )

    def relay_copy(h, part):
        return pltpu.make_async_remote_copy(
            src_ref=piece(d, part, far_row(d), h), dst_ref=piece(d, part, 128, h),
            send_sem=rel_send.at[h, part], recv_sem=rel_recv.at[h, part],
            device_id=sib, device_id_type=MESH,
        )

    def chip_copy(part):
        return pltpu.make_async_remote_copy(
            src_ref=wide.at[e, part, pl.ds(own_row(e), 128)],
            dst_ref=wide.at[e, part, pl.ds(128, 128)],
            send_sem=chip_send.at[part], recv_sem=chip_recv.at[part],
            device_id=sib, device_id_type=MESH,
        )

    def start_first(h, carry):
        first_copy(h, 0).start()
        first_copy(h, 1).start()
        return carry

    lax.fori_loop(0, H, start_first, 0)
    chip_copy(0).start()
    chip_copy(1).start()

    def block(side, h, lo, width):
        cols = head_cols(h)
        rows = pl.ds(lo, width)
        other = 1 - side
        own = pl.ds(own_row(other), 128)
        x3 = wide[side, 0, rows, cols]
        y3 = wide[side, 1, rows, cols]
        y = nt(wide[other, 0, own, cols], x3) * (0.5 * SCALE) + toep[side, h, :, rows]
        pulled = nt(wide[other, 1, own, cols], y3)
        t = jnp.tanh(y)
        w0 = y * t + y
        sg = 0.5 * t + 0.5
        mk = mask[side, :, rows]
        weights = (w0 * mk).astype(BF16)
        slopes = pulled * (sg + w0 * (1.0 - sg)) * mk
        o1 = jnp.dot(weights, y3, preferred_element_type=F32)
        o2 = jnp.dot(slopes.astype(BF16), x3, preferred_element_type=F32) * SCALE
        return o1, o2, slopes

    chip_copy(0).wait_recv()
    chip_copy(1).wait_recv()

    def other_near(h):
        relay_copy(h, 0).wait_recv()
        relay_copy(h, 1).wait_recv()
        o1, o2, slopes = block(e, h, pl.multiple_of(128 * (1 - e), 128), 256)
        acc[0, :, head_cols(h)] = o1
        acc[1, :, head_cols(h)] = o2

        @pl.when(c == 1)
        def _():
            near = slopes[:, 128:256]
            diag = diagonals(jnp.concatenate([jnp.zeros_like(near), near], axis=1), 256)
            total = jnp.sum(diag, axis=0, keepdims=True)
            bl[3 * h] = bl[3 * h] + total[:, :128]
            bl[3 * h + 1] = bl[3 * h + 1] + total[:, 128:]

    keep_near = jnp.where(c == 0, 1.0, 0.0).astype(F32)

    def direct(h, carry):
        for part in range(2):
            first_copy(h, part).wait_recv()
            relay_copy(h, part).start()
        o1, o2, slopes = block(d, h, 0, 384)
        outb[d, 0, :, head_cols(h)] = o1.astype(BF16)
        outb[d, 1, :, head_cols(h)] = o2.astype(BF16)
        framed = jnp.concatenate(
            [slopes[:, :128], slopes[:, 128:256] * keep_near, slopes[:, 256:], jnp.zeros((128, 128), F32)],
            axis=1,
        )
        diag = diagonals(framed, 512)
        back = pltpu.roll(diag, 511, 1)
        source = (1, 0, 3)
        for k in range(3):
            straight = diag[:, 128 * k : 128 * k + 128]
            turned = flip(back[:, 128 * source[k] : 128 * source[k] + 128])
            total = jnp.where(jnp.full((8, 128), c) == 0, straight, turned)
            bl[3 * h + k] = jnp.sum(total, axis=0, keepdims=True)

        @pl.when(h > 0)
        def _():
            other_near(h - 1)

        return carry

    lax.fori_loop(0, H, direct, 0)

    def start_second(h, carry):
        for part in range(2):
            first_copy(h, part).wait_send()
            second_copy(h, part).start()
        return carry

    lax.fori_loop(0, H, start_second, 0)
    direct_out = pltpu.make_async_copy(outb.at[d], res_ref.at[d], out_sem.at[0])
    direct_out.start()
    other_near(H - 1)

    def ar_copy(step, src, dst, device):
        return pltpu.make_async_remote_copy(
            src_ref=src, dst_ref=dst, send_sem=ar_send.at[step], recv_sem=ar_recv.at[step],
            device_id=device, device_id_type=MESH,
        )

    def finish(lo, hi):
        def body(h, carry):
            for part in range(2):
                second_copy(h, part).wait_recv()
            o1, o2, _ = block(e, h, far_row(e), 128)
            outb[e, 0, :, head_cols(h)] = (acc[0, :, head_cols(h)] + o1).astype(BF16)
            outb[e, 1, :, head_cols(h)] = (acc[1, :, head_cols(h)] + o2).astype(BF16)
            return carry

        lax.fori_loop(lo, hi, body, 0)

    def send_rows(j, carry):
        k = (m + j) % 24
        ar_copy(0, bl.at[k], r1.at[m], line_peer(j)).start()
        return carry

    lax.fori_loop(1, 24, send_rows, 0)
    r1[m] = bl[m]
    finish(0, 2)
    ar_copy(0, bl.at[pl.ds(0, 23)], r1.at[pl.ds(0, 23)], sib).wait()
    me = x * n_grp + grp
    r2[me] = jnp.sum(r1[...], axis=0)

    def send_sums(j, carry):
        ar_copy(1, r2.at[me], r2.at[me], plane_peer(j)).start()
        return carry

    lax.fori_loop(1, 32, send_sums, 0)
    finish(2, 5)
    ar_copy(1, r2.at[pl.ds(0, 31)], r2.at[pl.ds(0, 31)], sib).wait()
    fin[m] = jnp.sum(r2[...], axis=0) * (n_seq * n_grp) ** (-0.5)

    def send_done(j, carry):
        ar_copy(2, fin.at[m], fin.at[m], line_peer(j)).start()
        return carry

    lax.fori_loop(1, 24, send_done, 0)
    finish(5, H)
    other_out = pltpu.make_async_copy(outb.at[e], res_ref.at[e], out_sem.at[1])
    other_out.start()
    ar_copy(2, fin.at[pl.ds(0, 23)], fin.at[pl.ds(0, 23)], sib).wait()
    for h in range(H):
        for k in range(3):
            bg_ref[h : h + 1, 128 * k : 128 * k + 128] = fin[3 * h + k]

    for part in range(2):
        chip_copy(part).wait_send()

    def drain(h, carry):
        for part in range(2):
            relay_copy(h, part).wait_send()
            second_copy(h, part).wait_send()
        return carry

    lax.fori_loop(0, H, drain, 0)
    direct_out.wait()
    other_out.wait()


def copy_kernel(res_ref, bg_ref, att_ref, qg_ref, kg_ref, vg_ref, bias_ref, sem):
    copies = []
    for i, (side, part, ref) in enumerate(
        ((0, 0, att_ref), (0, 1, qg_ref), (1, 1, kg_ref), (1, 0, vg_ref))
    ):
        copy = pltpu.make_async_copy(res_ref.at[side, part], ref.at[0], sem.at[i])
        copy.start()
        copies.append(copy)
    bias_ref[...] = bg_ref[...]
    for copy in copies:
        copy.wait()


def on_device(queries, key_rows, value_rows, out_grad, positions, user_len, position_bias):
    any_spec = pl.BlockSpec(memory_space=pl.ANY)
    vmem = pl.BlockSpec(memory_space=pltpu.VMEM)
    smem = pl.BlockSpec(memory_space=pltpu.SMEM)
    dma = pltpu.SemaphoreType.DMA
    res, bg = pl.pallas_call(
        main_kernel,
        out_shape=(
            jax.ShapeDtypeStruct((2, 2, BLOCK, D), BF16),
            jax.ShapeDtypeStruct((H, 384), F32),
        ),
        in_specs=[any_spec] * 4 + [smem, smem, vmem],
        out_specs=(any_spec, vmem),
        scratch_shapes=[
            pltpu.VMEM((2, 2, 384, D), BF16),
            pltpu.VMEM((2, H, 128, 384), F32),
            pltpu.VMEM((2, 128, 384), F32),
            pltpu.VMEM((2, 2, 128, D), BF16),
            pltpu.VMEM((2, 128, D), F32),
            pltpu.VMEM((24, 1, 128), F32),
            pltpu.VMEM((24, 1, 128), F32),
            pltpu.VMEM((32, 1, 128), F32),
            pltpu.VMEM((24, 1, 128), F32),
            dma((4,)),
            dma((2,)),
            dma((2,)),
            dma((H, 2)),
            dma((H, 2)),
            dma((H, 2)),
            dma((H, 2)),
            dma((H, 2)),
            dma((H, 2)),
            dma((3,)),
            dma((3,)),
            dma((2,)),
        ],
        compiler_params=pltpu.CompilerParams(
            collective_id=0, has_side_effects=True, vmem_limit_bytes=48 * 1024 * 1024
        ),
        name="attention",
    )(queries, key_rows, value_rows, out_grad, positions, user_len, position_bias)
    whole = jax.ShapeDtypeStruct((1, BLOCK, D), BF16)
    return pl.pallas_call(
        copy_kernel,
        out_shape=(whole, whole, whole, whole, jax.ShapeDtypeStruct((H, 384), F32)),
        in_specs=[any_spec, vmem],
        out_specs=(any_spec, any_spec, any_spec, any_spec, vmem),
        scratch_shapes=[dma((4,))],
        name="results",
    )(res, bg)


def solution(mesh):
    return jax.shard_map(
        on_device,
        mesh=mesh,
        in_specs=(
            P("grp", "seq", None),
            P("grp", "seq", None),
            P("grp", "seq", None),
            P("grp", "seq", None),
            P("grp", "seq"),
            P("grp", "seq"),
            P(),
        ),
        out_specs=(
            P("grp", "seq", None),
            P("grp", "seq", None),
            P("grp", "seq", None),
            P("grp", "seq", None),
            P(),
        ),
        check_vma=False,
    )
```

time: 194 us -> 101 us (0.52)
  blocking collectives: 130 us -> 0 us
  Pallas kernels: 0 us -> 93.1 us
  starting transfers between devices: 22.8 us -> 0 us
  local copies, waits for them, and re-layouts: 22.3 us -> 6.05 us
  matrix products: 9.12 us -> 0 us
  other arithmetic: 5.2 us -> 0 us
    psum x1 -> x0, blocking collectives: 130 us -> none  [on_device(): summed = lax.psum(totals[4], ('seq', 'grp'))]
    pallas_call x0 -> x2, Pallas kernels: none -> 93.1 us  [the longest x1 58.9 us: on_device(): pl.pallas_call(main_kernel, out_shape=(jax.ShapeDtypeStruct((2, 2, BLOCK,...]
    ppermute x8 -> x0, starting transfers between devices: 22.8 us -> none  [passed_along(): return lax.ppermute(block, axis, route)]
    dot_general x12 -> x0, matrix products: 9.12 us -> none  [the longest x2 2.32 us: compute(): jnp.einsum('hrc,chd->rhd', weights, value_heads, preferred_element_type=j...]
    reshape x6 -> x0, local copies, waits for them, and re-layouts: 6.05 us -> none  [the longest x4 4.02 us: toeplitz(): tiling.reshape(bias_table.shape[0], block_rows, 2 * block_rows - 1)]
    cond x10 -> x0, local copies, waits for them, and re-layouts: 3.73 us -> none  [the longest x4 2.94 us: pair_terms(): return lax.cond(active, compute, skipped, None)]
    mul x4 -> x0, local copies, waits for them, and re-layouts: 3.71 us -> none  [the longest x2 1.86 us: compute(): jnp.einsum('hrc,chd->rhd', slopes_low, key_heads, preferred_element_type=...]
    broadcast_in_dim x2 -> x0, other arithmetic: 2.55 us -> none  [the longest x1 1.75 us: on_device(): totals[3].astype(jnp.bfloat16)[None]]
  transfers between devices with their start and end apart: 8 -> 0, of which waited for: 0 -> 0; matrix products, arithmetic and copies ran while one was open for 16% -> 0% of each run, Pallas kernels for 0% -> 0%
where the time goes in v1:
time: 101 us
  Pallas kernels  93.1 us (92%)
  local copies, waits for them, and re-layouts  6.05 us (6%)
  between operations  1.95 us (2%)
    pallas_call x1, Pallas kernels, on_device(): pl.pallas_call(main_kernel, out_shape=(jax.ShapeDtypeStruct((2, 2, BLOCK,...  58.9 us
    pallas_call x1, Pallas kernels, on_device(): pl.pallas_call(copy_kernel, out_shape=(whole, whole, whole, whole, jax.Sh...  34.2 us
    unnamed x14, local copies, waits for them, and re-layouts  6.05 us

profile of v1, /device:TPU:1, one launch (start us, length us, event | category | flops | bytes accessed | tf_op | source)
XLA Modules:
  0.0 101.1 jit_solution(1488805174245732494)
XLA Ops:
  1.9 0.0 copy-start.1
  1.9 0.9 copy-done.1
  2.9 0.0 copy-start.2
  2.9 0.9 copy-done.2
  3.8 0.0 copy-start.3
  3.8 0.9 copy-done.3
  4.8 0.0 copy-start.4
  4.8 0.9 copy-done.4
  5.7 0.0 copy-start.5
  5.7 0.7 copy-done.5
  6.4 58.9 %attention.1 = (bf16[2,2,128,1024]{3,2,1,0:T(8,128)(2,1)S(1)}, f32[8,384]{1,0:T(8,128)S(1)}) custom-call(bf16[1,128,1024]{2,1,0:T(8,128)(2,1)S(1)} %copy-done.1, bf16[1,128,1024]{2,1,0:T(8,128)(2,1)S(1)} %copy-done.2, bf16[1,128,1024]{2,1,0:T(8,128)(2,1)S(1)} %copy-done.3, bf16[1,128,1024]{2,1,0:T(8,128)(2,1)S(1)} %copy-done.4, s32[1,1]{1,0:T(1,128)S(6)} %copy.12.pos_ref, ...), custom_call_target="tpu_custom_call" | custom-call | tf_op jit(solution)/shard_map/attention/pallas_call | solution.py:344
  65.3 0.0 copy-start
  65.3 1.0 copy-done
  66.3 0.0 copy-start.6
  66.3 0.6 copy-done.6
  66.9 34.2 %results.1 = (bf16[1,128,1024]{2,1,0:T(8,128)(2,1)}, bf16[1,128,1024]{2,1,0:T(8,128)(2,1)}, bf16[1,128,1024]{2,1,0:T(8,128)(2,1)}, bf16[1,128,1024]{2,1,0:T(8,128)(2,1)}, f32[8,384]{1,0:T(8,128)}) custom-call(bf16[2,2,128,1024]{3,2,1,0:T(8,128)(2,1)} %copy-done, f32[8,384]{1,0:T(8,128)} %copy-done.6), custom_call_target="tpu_custom_call" | custom-call | tf_op jit(solution)/shard_map/results/pallas_call | solution.py:381
Async XLA Ops:
  1.9 1.0 copy-start.1
  2.9 0.9 copy-start.2
  3.8 0.9 copy-start.3
  4.8 0.9 copy-start.4
  5.7 0.7 copy-start.5
  65.3 1.0 copy-start
  66.3 0.6 copy-start.6

commit v2 on v1

v2 whole, which is shorter than its diff:
```python
import jax
import jax.numpy as jnp
from jax import lax
from jax.experimental import pallas as pl
from jax.experimental.pallas import tpu as pltpu
from jax.sharding import PartitionSpec as P

H = 8
BLOCK = 128
D = 1024
MESH = pl.DeviceIdType.MESH
F32 = jnp.float32
BF16 = jnp.bfloat16
SCALE = 128 ** -0.5


def own_row(side):
    return pl.multiple_of(256 * (1 - side), 128)


def far_row(side):
    return pl.multiple_of(256 * side, 128)


def head_cols(h):
    return pl.ds(pl.multiple_of(h * 128, 128), 128)


def flip(x):
    lane = lax.broadcasted_iota(jnp.int32, x.shape, 1)
    return jnp.take_along_axis(x, 127 - lane, axis=1, mode="promise_in_bounds")


def skew(x, left):
    width = x.shape[1]
    row = lax.broadcasted_iota(jnp.int32, x.shape, 0)
    for bit in (1, 2, 4):
        moved = pltpu.roll(x, width - bit if left else bit, 1)
        x = jnp.where((row & bit) != 0, moved, x)
    return x


def nt(a, b):
    return lax.dot_general(a, b, (((1,), (1,)), ((), ())), preferred_element_type=F32)


def diagonals(slopes, width):
    total = None
    for i in range(16):
        slab = slopes[8 * i : 8 * i + 8]
        if i:
            slab = pltpu.roll(slab, width - 8 * i, 1)
        total = slab if total is None else total + slab
    return skew(total, True)


def main_kernel(
    q_ref, k_ref, v_ref, g_ref, pos_ref, len_ref, bias_ref,
    res_ref, bg_ref,
    wide, toep, mask, bias, place, acc, bl, r1, r2, fin,
    load_sem, chip_send, chip_recv, w1_send, w1_recv, rel_send, rel_recv, w2_send, w2_recv,
    up_send, up_recv, flat_send, flat_recv, down_send, down_recv, small_sem,
):
    s = lax.axis_index("seq")
    grp = lax.axis_index("grp")
    n_seq = lax.axis_size("seq")
    n_grp = lax.axis_size("grp")
    c = s % 2
    x = s // 24
    m = s % 24
    d = 1 - c
    e = c
    sib = {"seq": s + 1 - 2 * c, "grp": grp}
    ahead = {"seq": (s + 4 * c - 2 + n_seq) % n_seq, "grp": grp}
    behind = {"seq": (s + 2 - 4 * c + n_seq) % n_seq, "grp": grp}

    smalls = []
    for i, (src, dst) in enumerate(
        ((bias_ref, bias), (pos_ref, place.at[pl.ds(0, 1)]), (len_ref, place.at[pl.ds(1, 1)]))
    ):
        copy = pltpu.make_async_copy(src, dst, small_sem.at[i])
        copy.start()
        smalls.append(copy)
    loads = []
    for i, (ref, side, part) in enumerate(
        ((q_ref, 1, 0), (g_ref, 1, 1), (k_ref, 0, 0), (v_ref, 0, 1))
    ):
        row = 256 * (1 - side)
        copy = pltpu.make_async_copy(
            ref.at[0], wide.at[side, part, pl.ds(row, 128)], load_sem.at[i]
        )
        copy.start()
        loads.append(copy)

    barrier = pltpu.get_barrier_semaphore()

    def greet(device):
        pl.semaphore_signal(barrier, inc=1, device_id=device, device_id_type=MESH)

    def line_peer(j):
        return {"seq": s - m + j, "grp": grp}

    def plane_peer(j):
        t = (x * n_grp + grp + j) % 32
        return {"seq": (t // n_grp) * 24 + m, "grp": t % n_grp}

    adds = m < 2
    greet(ahead)
    greet(behind)
    greet(sib)

    @pl.when(adds)
    def _():
        for j in range(1, 32):
            greet(plane_peer(j))
        for j in range(2, 24):
            greet(line_peer(j))

    for copy in loads:
        copy.wait()

    @pl.when(adds)
    def _():
        pl.semaphore_wait(barrier, 3 + 31)

    @pl.when(jnp.logical_not(adds))
    def _():
        pl.semaphore_wait(barrier, 3 + 2)

    def piece(side, part, rows, h):
        return wide.at[side, part, pl.ds(rows, 128), head_cols(h)]

    def first_copy(h, part):
        return pltpu.make_async_remote_copy(
            src_ref=piece(d, part, own_row(d), h), dst_ref=piece(d, part, far_row(d), h),
            send_sem=w1_send.at[h, part], recv_sem=w1_recv.at[h, part],
            device_id=ahead, device_id_type=MESH,
        )

    def second_copy(h, part):
        return pltpu.make_async_remote_copy(
            src_ref=piece(e, part, own_row(e), h), dst_ref=piece(e, part, far_row(e), h),
            send_sem=w2_send.at[h, part], recv_sem=w2_recv.at[h, part],
            device_id=behind, device_id_type=MESH,
        )

    def relay_copy(h, part):
        return pltpu.make_async_remote_copy(
            src_ref=piece(d, part, far_row(d), h), dst_ref=piece(d, part, 128, h),
            send_sem=rel_send.at[h, part], recv_sem=rel_recv.at[h, part],
            device_id=sib, device_id_type=MESH,
        )

    def chip_copy(part):
        return pltpu.make_async_remote_copy(
            src_ref=wide.at[e, part, pl.ds(own_row(e), 128)],
            dst_ref=wide.at[e, part, pl.ds(128, 128)],
            send_sem=chip_send.at[part], recv_sem=chip_recv.at[part],
            device_id=sib, device_id_type=MESH,
        )

    def start_first(h, carry):
        first_copy(h, 0).start()
        first_copy(h, 1).start()
        return carry

    lax.fori_loop(0, H, start_first, 0)
    chip_copy(0).start()
    chip_copy(1).start()

    for copy in smalls:
        copy.wait()
    p = place[0, 0]
    n = place[1, 0]
    row = lax.broadcasted_iota(jnp.int32, (128, 384), 0)
    lane = lax.broadcasted_iota(jnp.int32, (128, 384), 1)
    inverse = 1.0 / jnp.full((128, 384), n, jnp.int32).astype(F32)
    used = (row < n - p * 128) & (lane >= 256 - 128 * p) & (lane <= 256 + row)
    mask[0] = jnp.where(used, inverse, 0.0)
    used = (lane < n - p * 128) & (lane >= row)
    mask[1] = jnp.where(used, inverse, 0.0)

    def make_toep(h, carry):
        b = jnp.broadcast_to(bias[pl.ds(h, 1), :] * 0.5, (8, 384))
        b0, b1, b2 = b[:, :128], b[:, 128:256], b[:, 256:]
        zero = jnp.zeros_like(b0)
        keyed = skew(jnp.concatenate([b0, b1, b2, zero], axis=1), False)
        quer = jnp.concatenate([flip(b1), flip(b0), zero, flip(b2)], axis=1)
        quer = skew(pltpu.roll(quer, 1, 1), False)
        for i in range(16):
            toep[1, h, 8 * i : 8 * i + 8, :] = (pltpu.roll(keyed, 8 * i, 1) if i else keyed)[:, :384]
            toep[0, h, 8 * i : 8 * i + 8, :] = (pltpu.roll(quer, 8 * i, 1) if i else quer)[:, :384]
        return carry

    lax.fori_loop(0, H, make_toep, 0)

    def block(side, h, lo, width):
        cols = head_cols(h)
        rows = pl.ds(lo, width)
        other = 1 - side
        own = pl.ds(own_row(other), 128)
        x3 = wide[side, 0, rows, cols]
        y3 = wide[side, 1, rows, cols]
        y = nt(wide[other, 0, own, cols], x3) * (0.5 * SCALE) + toep[side, h, :, rows]
        pulled = nt(wide[other, 1, own, cols], y3)
        t = jnp.tanh(y)
        w0 = y * t + y
        sg = 0.5 * t + 0.5
        mk = mask[side, :, rows]
        weights = (w0 * mk).astype(BF16)
        slopes = pulled * (sg + w0 * (1.0 - sg)) * mk
        o1 = jnp.dot(weights, y3, preferred_element_type=F32)
        o2 = jnp.dot(slopes.astype(BF16), x3, preferred_element_type=F32) * SCALE
        return o1, o2, slopes

    chip_copy(0).wait_recv()
    chip_copy(1).wait_recv()

    def other_near(h):
        relay_copy(h, 0).wait_recv()
        relay_copy(h, 1).wait_recv()
        o1, o2, slopes = block(e, h, pl.multiple_of(128 * (1 - e), 128), 256)
        acc[0, :, head_cols(h)] = o1
        acc[1, :, head_cols(h)] = o2

        @pl.when(c == 1)
        def _():
            near = slopes[:, 128:256]
            diag = diagonals(jnp.concatenate([jnp.zeros_like(near), near], axis=1), 256)
            total = jnp.sum(diag, axis=0, keepdims=True)
            bl[3 * h] = bl[3 * h] + total[:, :128]
            bl[3 * h + 1] = bl[3 * h + 1] + total[:, 128:]

    keep_near = jnp.where(c == 0, 1.0, 0.0).astype(F32)

    def direct(h, carry):
        for part in range(2):
            first_copy(h, part).wait_recv()
            relay_copy(h, part).start()
        o1, o2, slopes = block(d, h, 0, 384)
        res_ref[d, 0, :, head_cols(h)] = o1.astype(BF16)
        res_ref[d, 1, :, head_cols(h)] = o2.astype(BF16)
        framed = jnp.concatenate(
            [slopes[:, :128], slopes[:, 128:256] * keep_near, slopes[:, 256:], jnp.zeros((128, 128), F32)],
            axis=1,
        )
        diag = diagonals(framed, 512)
        back = pltpu.roll(diag, 511, 1)
        source = (1, 0, 3)
        for k in range(3):
            straight = diag[:, 128 * k : 128 * k + 128]
            turned = flip(back[:, 128 * source[k] : 128 * source[k] + 128])
            total = jnp.where(jnp.full((8, 128), c) == 0, straight, turned)
            bl[3 * h + k] = jnp.sum(total, axis=0, keepdims=True)

        @pl.when(h > 0)
        def _():
            other_near(h - 1)

        return carry

    me = x * n_grp + grp

    def rows_of(group, half):
        return pl.ds(9 * half, 9) if group == 0 else pl.ds(18 + 3 * half, 3)

    part_of = (pl.ds(0, 9), pl.ds(9, 3))

    def up_copy(group, half):
        return pltpu.make_async_remote_copy(
            src_ref=bl.at[rows_of(group, half)], dst_ref=r1.at[m, part_of[group]],
            send_sem=up_send, recv_sem=up_recv.at[group],
            device_id=line_peer(half), device_id_type=MESH,
        )

    def flat_copy(group, j):
        return pltpu.make_async_remote_copy(
            src_ref=r2.at[me, part_of[group]], dst_ref=r2.at[me, part_of[group]],
            send_sem=flat_send, recv_sem=flat_recv.at[group],
            device_id=plane_peer(j), device_id_type=MESH,
        )

    def down_copy(group, j):
        return pltpu.make_async_remote_copy(
            src_ref=fin.at[rows_of(group, c)], dst_ref=fin.at[rows_of(group, c)],
            send_sem=down_send, recv_sem=down_recv,
            device_id=line_peer(j), device_id_type=MESH,
        )

    def bytes_of(ref, send_sem, recv_sem):
        return pltpu.make_async_remote_copy(
            src_ref=ref, dst_ref=ref, send_sem=send_sem, recv_sem=recv_sem,
            device_id=sib, device_id_type=MESH,
        )

    def send_up(group):
        @pl.when(adds)
        def _():
            up_copy(group, 1 - c).start()
            r1[m, part_of[group]] = bl[rows_of(group, c)]

        @pl.when(jnp.logical_not(adds))
        def _():
            up_copy(group, 0).start()
            up_copy(group, 1).start()

    def add_line(group):
        part = part_of[group]
        others = r1.at[pl.ds(0, 23), part]
        bytes_of(others, up_send, up_recv.at[group]).wait_recv()
        r2[me, part] = jnp.sum(r1[:, part], axis=0)
        for j in range(1, 32):
            flat_copy(group, j).start()

    def add_plane(group):
        part = part_of[group]
        others = r2.at[pl.ds(0, 31), part]
        bytes_of(others, flat_send, flat_recv.at[group]).wait_recv()
        fin[rows_of(group, c)] = jnp.sum(r2[:, part], axis=0) * (n_seq * n_grp) ** (-0.5)
        down_copy(group, 1 - c).start()
        for j in range(2, 24):
            down_copy(group, j).start()

    lax.fori_loop(0, 7, direct, 0)
    send_up(0)
    direct(7, 0)
    other_near(7)
    send_up(1)

    def start_second(h, carry):
        for part in range(2):
            first_copy(h, part).wait_send()
            second_copy(h, part).start()
        return carry

    lax.fori_loop(0, H, start_second, 0)

    @pl.when(adds)
    def _():
        add_line(0)
        add_line(1)

    def finish(h, carry):
        for part in range(2):
            second_copy(h, part).wait_recv()
        o1, o2, _ = block(e, h, far_row(e), 128)
        res_ref[e, 0, :, head_cols(h)] = (acc[0, :, head_cols(h)] + o1).astype(BF16)
        res_ref[e, 1, :, head_cols(h)] = (acc[1, :, head_cols(h)] + o2).astype(BF16)
        return carry

    lax.fori_loop(0, H, finish, 0)
    for part in range(2):
        chip_copy(part).wait_send()

    def drain(h, carry):
        for part in range(2):
            relay_copy(h, part).wait_send()
            second_copy(h, part).wait_send()
        return carry

    lax.fori_loop(0, H, drain, 0)

    @pl.when(adds)
    def _():
        add_plane(0)
        add_plane(1)
        bytes_of(r1.at[0], up_send, down_recv).wait()
        bytes_of(r2.at[pl.ds(0, 31)], flat_send, down_recv).wait_send()
        bytes_of(r1.at[pl.ds(0, 23)], down_send, down_recv).wait_send()

    @pl.when(jnp.logical_not(adds))
    def _():
        bytes_of(fin, up_send, down_recv).wait()

    for h in range(H):
        for k in range(3):
            bg_ref[h : h + 1, 128 * k : 128 * k + 128] = fin[3 * h + k]


def copy_kernel(res_ref, bg_ref, att_ref, qg_ref, kg_ref, vg_ref, bias_ref, sem):
    copies = []
    for i, (side, part, ref) in enumerate(
        ((0, 0, att_ref), (0, 1, qg_ref), (1, 1, kg_ref), (1, 0, vg_ref))
    ):
        copy = pltpu.make_async_copy(res_ref.at[side, part], ref.at[0], sem.at[i])
        copy.start()
        copies.append(copy)
    copy = pltpu.make_async_copy(bg_ref, bias_ref, sem.at[4])
    copy.start()
    copies.append(copy)
    for copy in copies:
        copy.wait()


def on_device(queries, key_rows, value_rows, out_grad, positions, user_len, position_bias):
    hbm = pl.BlockSpec(memory_space=pltpu.HBM)
    vmem = pl.BlockSpec(memory_space=pltpu.VMEM)
    dma = pltpu.SemaphoreType.DMA
    res, bg = pl.pallas_call(
        main_kernel,
        out_shape=(
            jax.ShapeDtypeStruct((2, 2, BLOCK, D), BF16),
            jax.ShapeDtypeStruct((H, 384), F32),
        ),
        in_specs=[hbm] * 7,
        out_specs=(vmem, vmem),
        scratch_shapes=[
            pltpu.VMEM((2, 2, 384, D), BF16),
            pltpu.VMEM((2, H, 128, 384), F32),
            pltpu.VMEM((2, 128, 384), F32),
            pltpu.VMEM((H, 384), F32),
            pltpu.SMEM((2, 1), jnp.int32),
            pltpu.VMEM((2, 128, D), F32),
            pltpu.VMEM((24, 1, 128), F32),
            pltpu.VMEM((24, 12, 1, 128), F32),
            pltpu.VMEM((32, 12, 1, 128), F32),
            pltpu.VMEM((24, 1, 128), F32),
            dma((4,)),
            dma((2,)),
            dma((2,)),
            dma((H, 2)),
            dma((H, 2)),
            dma((H, 2)),
            dma((H, 2)),
            dma((H, 2)),
            dma((H, 2)),
            dma(()),
            dma((2,)),
            dma(()),
            dma((2,)),
            dma(()),
            dma(()),
            dma((3,)),
        ],
        compiler_params=pltpu.CompilerParams(
            collective_id=0, has_side_effects=True, vmem_limit_bytes=32 * 1024 * 1024
        ),
        name="attention",
    )(*(pltpu.with_memory_space_constraint(a, pltpu.HBM) for a in (queries, key_rows, value_rows, out_grad)), positions, user_len, pltpu.with_memory_space_constraint(position_bias, pltpu.HBM))
    whole = jax.ShapeDtypeStruct((1, BLOCK, D), BF16)
    return pl.pallas_call(
        copy_kernel,
        out_shape=(whole, whole, whole, whole, jax.ShapeDtypeStruct((H, 384), F32)),
        in_specs=[vmem, vmem],
        out_specs=(hbm,) * 5,
        scratch_shapes=[dma((5,))],
        compiler_params=pltpu.CompilerParams(vmem_limit_bytes=4 * 1024 * 1024),
        name="results",
    )(res, bg)


def solution(mesh):
    return jax.shard_map(
        on_device,
        mesh=mesh,
        in_specs=(
            P("grp", "seq", None),
            P("grp", "seq", None),
            P("grp", "seq", None),
            P("grp", "seq", None),
            P("grp", "seq"),
            P("grp", "seq"),
            P(),
        ),
        out_specs=(
            P("grp", "seq", None),
            P("grp", "seq", None),
            P("grp", "seq", None),
            P("grp", "seq", None),
            P(),
        ),
        check_vma=False,
    )
```

time: 101 us -> 49.7 us (0.49)
  Pallas kernels: 93.1 us -> 47.6 us
  local copies, waits for them, and re-layouts: 6.05 us -> 0 us
    pallas_call x1, Pallas kernels: 34.2 us -> 1.01 us  [on_device(): pl.pallas_call(copy_kernel, out_shape=(whole, whole, whole, whole, jax.Sh...]
    pallas_call x1, Pallas kernels: 58.9 us -> 46.6 us  [on_device(): pl.pallas_call(main_kernel, out_shape=(jax.ShapeDtypeStruct((2, 2, BLOCK,...]
    unnamed x14 -> x0, local copies, waits for them, and re-layouts: 6.05 us -> none
where the time goes in v2:
time: 49.7 us; the launch traced here: 49.6 us
  Pallas kernels  47.6 us (96%)
  between operations  1.93 us (4%)
    pallas_call x1, Pallas kernels, on_device(): pl.pallas_call(main_kernel, out_shape=(jax.ShapeDtypeStruct((2, 2, BLOCK,...  46.6 us
    pallas_call x1, Pallas kernels, on_device(): pl.pallas_call(copy_kernel, out_shape=(whole, whole, whole, whole, jax.Sh...  1.01 us

profile of v2, /device:TPU:1, one launch (start us, length us, event | category | flops | bytes accessed | tf_op | source)
XLA Modules:
  0.0 49.6 jit_solution(2462997601778850995)
XLA Ops:
  1.9 46.6 %attention.1 = (bf16[2,2,128,1024]{3,2,1,0:T(8,128)(2,1)S(1)}, f32[8,384]{1,0:T(8,128)S(1)}) custom-call(bf16[1,128,1024]{2,1,0:T(8,128)(2,1)} %q_ref.1, bf16[1,128,1024]{2,1,0:T(8,128)(2,1)} %k_ref.1, bf16[1,128,1024]{2,1,0:T(8,128)(2,1)} %v_ref.1, bf16[1,128,1024]{2,1,0:T(8,128)(2,1)} %g_ref.1, s32[1,1]{1,0:T(1,128)S(6)} %copy.12.pos_ref, ...), custom_call_target="tpu_custom_call" | custom-call | tf_op jit(solution)/shard_map/attention/pallas_call | solution.py:399
  48.5 1.0 %results.1 = (bf16[1,128,1024]{2,1,0:T(8,128)(2,1)}, bf16[1,128,1024]{2,1,0:T(8,128)(2,1)}, bf16[1,128,1024]{2,1,0:T(8,128)(2,1)}, bf16[1,128,1024]{2,1,0:T(8,128)(2,1)}, f32[8,384]{1,0:T(8,128)}) custom-call(bf16[2,2,128,1024]{3,2,1,0:T(8,128)(2,1)S(1)} %get-tuple-element.7.res_ref, f32[8,384]{1,0:T(8,128)S(1)} %get-tuple-element.8.bg_ref), custom_call_target="tpu_custom_call" | custom-call | tf_op jit(solution)/shard_map/results/pallas_call | solution.py:441

commit v3 on v2

--- a/solution.py
+++ b/solution.py
@@ -31,34 +31,47 @@
     return jnp.take_along_axis(x, 127 - lane, axis=1, mode="promise_in_bounds")
 
 
-def skew(x, left):
-    width = x.shape[1]
-    row = lax.broadcasted_iota(jnp.int32, x.shape, 0)
-    for bit in (1, 2, 4):
-        moved = pltpu.roll(x, width - bit if left else bit, 1)
-        x = jnp.where((row & bit) != 0, moved, x)
-    return x
+def rolled(chunks, left):
+    width = 128 - left
+    lane = lax.broadcasted_iota(jnp.int32, (8, 128), 1)
+    turned = [pltpu.roll(chunk, width, 1) for chunk in chunks]
+    return [
+        jnp.where(lane < width, turned[k], turned[(k + 1) % len(chunks)])
+        for k in range(len(chunks))
+    ]
 
 
 def nt(a, b):
     return lax.dot_general(a, b, (((1,), (1,)), ((), ())), preferred_element_type=F32)
 
 
-def diagonals(slopes, width):
-    total = None
+def diagonals(slopes, width, extra):
+    count = width // 128
+    slabs = []
     for i in range(16):
-        slab = slopes[8 * i : 8 * i + 8]
-        if i:
-            slab = pltpu.roll(slab, width - 8 * i, 1)
-        total = slab if total is None else total + slab
-    return skew(total, True)
+        chunks = [slopes[8 * i : 8 * i + 8, 128 * k : 128 * k + 128] for k in range(count)]
+        slabs.append(rolled(chunks + [jnp.zeros((8, 128), F32)], 8 * i + extra))
+    while len(slabs) > 1:
+        slabs = [
+            [a + b for a, b in zip(slabs[k], slabs[k + 1])] for k in range(0, len(slabs), 2)
+        ]
+    chunks = slabs[0]
+    row = lax.broadcasted_iota(jnp.int32, (8, 128), 0)
+    for bit in (1, 2, 4):
+        moved = rolled(chunks, bit)
+        chunks = [jnp.where((row & bit) != 0, b, a) for a, b in zip(chunks, moved)]
+    return chunks
+
+
+def row_sum(x):
+    return jnp.sum(x, axis=0, keepdims=True)
 
 
 def main_kernel(
     q_ref, k_ref, v_ref, g_ref, pos_ref, len_ref, bias_ref,
     res_ref, bg_ref,
-    wide, toep, mask, bias, place, acc, bl, r1, r2, fin,
-    load_sem, chip_send, chip_recv, w1_send, w1_recv, rel_send, rel_recv, w2_send, w2_recv,
+    wide, sibling, sibling_mask, toep, mask, bias, place, wts, slp, bl, r1, r2, fin,
+    load_sem, chip_send, chip_recv, extra_send, extra_recv, w1_send, w1_recv, rel_send, rel_recv, w2_send, w2_recv,
     up_send, up_recv, flat_send, flat_recv, down_send, down_recv, small_sem,
 ):
     s = lax.axis_index("seq")
@@ -74,6 +87,17 @@
     ahead = {"seq": (s + 4 * c - 2 + n_seq) % n_seq, "grp": grp}
     behind = {"seq": (s + 2 - 4 * c + n_seq) % n_seq, "grp": grp}
 
+    loads = []
+    for i, (ref, side, part) in enumerate(
+        ((q_ref, 1, 0), (g_ref, 1, 1), (k_ref, 0, 0), (v_ref, 0, 1))
+    ):
+        row = 256 * (1 - side)
+        copy = pltpu.make_async_copy(
+            ref.at[0], wide.at[side, part, pl.ds(row, 128)], load_sem.at[i]
+        )
+        copy.start()
+        loads.append(copy)
+
     smalls = []
     for i, (src, dst) in enumerate(
         ((bias_ref, bias), (pos_ref, place.at[pl.ds(0, 1)]), (len_ref, place.at[pl.ds(1, 1)]))
@@ -81,17 +105,6 @@
         copy = pltpu.make_async_copy(src, dst, small_sem.at[i])
         copy.start()
         smalls.append(copy)
-    loads = []
-    for i, (ref, side, part) in enumerate(
-        ((q_ref, 1, 0), (g_ref, 1, 1), (k_ref, 0, 0), (v_ref, 0, 1))
-    ):
-        row = 256 * (1 - side)
-        copy = pltpu.make_async_copy(
-            ref.at[0], wide.at[side, part, pl.ds(row, 128)], load_sem.at[i]
-        )
-        copy.start()
-        loads.append(copy)
-
     barrier = pltpu.get_barrier_semaphore()
 
     def greet(device):
@@ -159,14 +172,30 @@
             device_id=sib, device_id_type=MESH,
         )
 
-    def start_first(h, carry):
+    for h in range(H):
         first_copy(h, 0).start()
         first_copy(h, 1).start()
-        return carry
-
-    lax.fori_loop(0, H, start_first, 0)
     chip_copy(0).start()
     chip_copy(1).start()
+
+    def extra_copy(part):
+        return pltpu.make_async_remote_copy(
+            src_ref=wide.at[0, part, pl.ds(256, 128)], dst_ref=sibling.at[part],
+            send_sem=extra_send.at[part], recv_sem=extra_recv.at[part],
+            device_id=sib, device_id_type=MESH,
+        )
+
+    def extra_mask():
+        return pltpu.make_async_remote_copy(
+            src_ref=mask.at[1, pl.ds(0, 8), pl.ds(128, 128)], dst_ref=sibling_mask,
+            send_sem=extra_send.at[2], recv_sem=extra_recv.at[2],
+            device_id=sib, device_id_type=MESH,
+        )
+
+    @pl.when(c == 1)
+    def _():
+        extra_copy(0).start()
+        extra_copy(1).start()
 
     for copy in smalls:
         copy.wait()
@@ -180,91 +209,123 @@
     used = (lane < n - p * 128) & (lane >= row)
     mask[1] = jnp.where(used, inverse, 0.0)
 
-    def make_toep(h, carry):
-        b = jnp.broadcast_to(bias[pl.ds(h, 1), :] * 0.5, (8, 384))
-        b0, b1, b2 = b[:, :128], b[:, 128:256], b[:, 256:]
-        zero = jnp.zeros_like(b0)
-        keyed = skew(jnp.concatenate([b0, b1, b2, zero], axis=1), False)
-        quer = jnp.concatenate([flip(b1), flip(b0), zero, flip(b2)], axis=1)
-        quer = skew(pltpu.roll(quer, 1, 1), False)
-        for i in range(16):
-            toep[1, h, 8 * i : 8 * i + 8, :] = (pltpu.roll(keyed, 8 * i, 1) if i else keyed)[:, :384]
-            toep[0, h, 8 * i : 8 * i + 8, :] = (pltpu.roll(quer, 8 * i, 1) if i else quer)[:, :384]
-        return carry
-
-    lax.fori_loop(0, H, make_toep, 0)
-
-    def block(side, h, lo, width):
+    def make_toep(side):
+        def body(h, carry):
+            b = jnp.broadcast_to(bias[pl.ds(h, 1), :] * 0.5, (8, 384))
+            b0, b1, b2 = b[:, :128], b[:, 128:256], b[:, 256:]
+            zero = jnp.zeros_like(b0)
+            keyed = jnp.concatenate([b0, b1, b2, zero], axis=1)
+            back = jnp.concatenate([flip(b1), flip(b0), zero, flip(b2)], axis=1)
+            base = jnp.where(side == 1, keyed, pltpu.roll(back, 1, 1))
+            base = jnp.broadcast_to(base[0:1], (128, 512))
+            toep[side, h] = pltpu.roll(base, 0, 1, stride=1, stride_axis=0)[:, :384]
+            return carry
+
+        lax.fori_loop(0, H, body, 0, unroll=2)
+
+    @pl.when(c == 1)
+    def _():
+        extra_mask().start()
+
+    make_toep(d)
+    make_toep(e)
+
+    def scores(side, h, lo, width):
         cols = head_cols(h)
         rows = pl.ds(lo, width)
         other = 1 - side
         own = pl.ds(own_row(other), 128)
-        x3 = wide[side, 0, rows, cols]
-        y3 = wide[side, 1, rows, cols]
-        y = nt(wide[other, 0, own, cols], x3) * (0.5 * SCALE) + toep[side, h, :, rows]
-        pulled = nt(wide[other, 1, own, cols], y3)
+        y = nt(wide[other, 0, own, cols], wide[side, 0, rows, cols])
+        y = y * (0.5 * SCALE) + toep[side, h, :, rows]
+        pulled = nt(wide[other, 1, own, cols], wide[side, 1, rows, cols])
         t = jnp.tanh(y)
         w0 = y * t + y
         sg = 0.5 * t + 0.5
         mk = mask[side, :, rows]
-        weights = (w0 * mk).astype(BF16)
         slopes = pulled * (sg + w0 * (1.0 - sg)) * mk
-        o1 = jnp.dot(weights, y3, preferred_element_type=F32)
-        o2 = jnp.dot(slopes.astype(BF16), x3, preferred_element_type=F32) * SCALE
-        return o1, o2, slopes
+        wts[side, h, :, rows] = (w0 * mk).astype(BF16)
+        slp[side, h, :, rows] = slopes.astype(BF16)
+        return slopes
+
+    def outputs(side, h):
+        cols = head_cols(h)
+        o1 = jnp.dot(wts[side, h], wide[side, 1, :, cols], preferred_element_type=F32)
+        o2 = jnp.dot(slp[side, h], wide[side, 0, :, cols], preferred_element_type=F32)
+        res_ref[side, 0, :, cols] = o1.astype(BF16)
+        res_ref[side, 1, :, cols] = (o2 * SCALE).astype(BF16)
+
+    def near_row(side):
+        return pl.multiple_of(128 * (1 - side), 128)
+
+    first_core = c == 0
+
+    def direct_near(h):
+        slopes = scores(d, h, near_row(d), 256)
+        lanes = lax.broadcasted_iota(jnp.int32, (128, 256), 1)
+        slopes = jnp.where(first_core | (lanes >= 128), slopes, 0.0)
+        n0, n1, _ = diagonals(slopes, 256, c)
+        bl[3 * h] = row_sum(jnp.where(first_core, n0, flip(n0)))
+        bl[3 * h + 1] = row_sum(n1)
+
+    def first_far(h):
+        cols = head_cols(h)
+        f0, f1 = diagonals(scores(1, h, 256, 128), 128, 0)
+        y = nt(sibling[0, :, cols], wide[1, 0, 256:, cols]) * (0.5 * SCALE) + toep[1, h, :, 128:256]
+        pulled = nt(sibling[1, :, cols], wide[1, 1, 256:, cols])
+        t = jnp.tanh(y)
+        w0 = y * t + y
+        sg = 0.5 * t + 0.5
+        slopes = pulled * (sg + w0 * (1.0 - sg)) * sibling_mask[0:1, :]
+        g0, g1 = diagonals(slopes, 128, 0)
+        bl[3 * h] = bl[3 * h] + row_sum(g1)
+        bl[3 * h + 1] = bl[3 * h + 1] + row_sum(f1 + g0)
+        bl[3 * h + 2] = row_sum(f0)
+
+    def second_far(h):
+        f0, f1 = diagonals(scores(0, h, 0, 128), 128, 1)
+        bl[3 * h + 1] = row_sum(flip(f0))
+        bl[3 * h + 2] = row_sum(flip(f1))
 
     chip_copy(0).wait_recv()
     chip_copy(1).wait_recv()
 
-    def other_near(h):
-        relay_copy(h, 0).wait_recv()
-        relay_copy(h, 1).wait_recv()
-        o1, o2, slopes = block(e, h, pl.multiple_of(128 * (1 - e), 128), 256)
-        acc[0, :, head_cols(h)] = o1
-        acc[1, :, head_cols(h)] = o2
+    def start_near(i, carry):
+        for h in range(4):
+            direct_near(4 * i + h)
+        return carry
+
+    lax.fori_loop(0, 2, start_near, 0)
+
+    @pl.when(c == 0)
+    def _():
+        for part in range(2):
+            extra_copy(part).wait_recv()
+        extra_mask().wait_recv()
+
+    def arrive(group):
+        heads = (2 * group, 2 * group + 1)
+        for h in heads:
+            for part in range(2):
+                first_copy(h, part).wait_recv()
+                relay_copy(h, part).start()
+
+        @pl.when(c == 0)
+        def _():
+            for h in heads:
+                first_far(h)
 
         @pl.when(c == 1)
         def _():
-            near = slopes[:, 128:256]
-            diag = diagonals(jnp.concatenate([jnp.zeros_like(near), near], axis=1), 256)
-            total = jnp.sum(diag, axis=0, keepdims=True)
-            bl[3 * h] = bl[3 * h] + total[:, :128]
-            bl[3 * h + 1] = bl[3 * h + 1] + total[:, 128:]
-
-    keep_near = jnp.where(c == 0, 1.0, 0.0).astype(F32)
-
-    def direct(h, carry):
-        for part in range(2):
-            first_copy(h, part).wait_recv()
-            relay_copy(h, part).start()
-        o1, o2, slopes = block(d, h, 0, 384)
-        res_ref[d, 0, :, head_cols(h)] = o1.astype(BF16)
-        res_ref[d, 1, :, head_cols(h)] = o2.astype(BF16)
-        framed = jnp.concatenate(
-            [slopes[:, :128], slopes[:, 128:256] * keep_near, slopes[:, 256:], jnp.zeros((128, 128), F32)],
-            axis=1,
-        )
-        diag = diagonals(framed, 512)
-        back = pltpu.roll(diag, 511, 1)
-        source = (1, 0, 3)
-        for k in range(3):
-            straight = diag[:, 128 * k : 128 * k + 128]
-            turned = flip(back[:, 128 * source[k] : 128 * source[k] + 128])
-            total = jnp.where(jnp.full((8, 128), c) == 0, straight, turned)
-            bl[3 * h + k] = jnp.sum(total, axis=0, keepdims=True)
-
-        @pl.when(h > 0)
-        def _():
-            other_near(h - 1)
-
-        return carry
+            for h in heads:
+                second_far(h)
 
     me = x * n_grp + grp
+    order = [8 * i + j for j in (0, 1, 2, 3, 7, 6, 4, 5) for i in (0, 2, 3, 1)]
 
     def rows_of(group, half):
-        return pl.ds(9 * half, 9) if group == 0 else pl.ds(18 + 3 * half, 3)
-
-    part_of = (pl.ds(0, 9), pl.ds(9, 3))
+        return pl.ds(6 * half, 6) if group == 0 else pl.ds(6 + 6 * group + 3 * half, 3)
+
+    part_of = (pl.ds(0, 6), pl.ds(6, 3), pl.ds(9, 3))
 
     def up_copy(group, half):
         return pltpu.make_async_remote_copy(
@@ -277,7 +338,7 @@
         return pltpu.make_async_remote_copy(
             src_ref=r2.at[me, part_of[group]], dst_ref=r2.at[me, part_of[group]],
             send_sem=flat_send, recv_sem=flat_recv.at[group],
-            device_id=plane_peer(j), device_id_type=MESH,
+            device_id={"seq": (j // 8) * 24 + m, "grp": j % 8}, device_id_type=MESH,
         )
 
     def down_copy(group, j):
@@ -309,8 +370,11 @@
         others = r1.at[pl.ds(0, 23), part]
         bytes_of(others, up_send, up_recv.at[group]).wait_recv()
         r2[me, part] = jnp.sum(r1[:, part], axis=0)
-        for j in range(1, 32):
-            flat_copy(group, j).start()
+        for j in order:
+
+            @pl.when(me != j)
+            def _(j=j):
+                flat_copy(group, j).start()
 
     def add_plane(group):
         part = part_of[group]
@@ -321,11 +385,13 @@
         for j in range(2, 24):
             down_copy(group, j).start()
 
-    lax.fori_loop(0, 7, direct, 0)
+    arrive(0)
+    arrive(1)
     send_up(0)
-    direct(7, 0)
-    other_near(7)
+    arrive(2)
     send_up(1)
+    arrive(3)
+    send_up(2)
 
     def start_second(h, carry):
         for part in range(2):
@@ -335,22 +401,40 @@
 
     lax.fori_loop(0, H, start_second, 0)
 
+    def rest(i, carry):
+        for h in range(2):
+            outputs(d, 2 * i + h)
+            for part in range(2):
+                relay_copy(2 * i + h, part).wait_recv()
+            scores(e, 2 * i + h, near_row(e), 256)
+        return carry
+
+    lax.fori_loop(0, H // 2, rest, 0)
+
     @pl.when(adds)
     def _():
-        add_line(0)
-        add_line(1)
-
-    def finish(h, carry):
-        for part in range(2):
-            second_copy(h, part).wait_recv()
-        o1, o2, _ = block(e, h, far_row(e), 128)
-        res_ref[e, 0, :, head_cols(h)] = (acc[0, :, head_cols(h)] + o1).astype(BF16)
-        res_ref[e, 1, :, head_cols(h)] = (acc[1, :, head_cols(h)] + o2).astype(BF16)
+        for group in range(3):
+            add_line(group)
+
+    def finish(i, carry):
+        for h in range(2):
+            for part in range(2):
+                second_copy(2 * i + h, part).wait_recv()
+        for h in range(2):
+            scores(e, 2 * i + h, far_row(e), 128)
+        for h in range(2):
+            outputs(e, 2 * i + h)
         return carry
 
-    lax.fori_loop(0, H, finish, 0)
+    lax.fori_loop(0, H // 2, finish, 0)
     for part in range(2):
         chip_copy(part).wait_send()
+
+    @pl.when(c == 1)
+    def _():
+        for part in range(2):
+            extra_copy(part).wait_send()
+        extra_mask().wait_send()
 
     def drain(h, carry):
         for part in range(2):
@@ -362,8 +446,8 @@
 
     @pl.when(adds)
     def _():
-        add_plane(0)
-        add_plane(1)
+        for group in range(3):
+            add_plane(group)
         bytes_of(r1.at[0], up_send, down_recv).wait()
         bytes_of(r2.at[pl.ds(0, 31)], flat_send, down_recv).wait_send()
         bytes_of(r1.at[pl.ds(0, 23)], down_send, down_recv).wait_send()
@@ -406,11 +490,14 @@
         out_specs=(vmem, vmem),
         scratch_shapes=[
             pltpu.VMEM((2, 2, 384, D), BF16),
+            pltpu.VMEM((2, 128, D), BF16),
+            pltpu.VMEM((8, 128), F32),
             pltpu.VMEM((2, H, 128, 384), F32),
             pltpu.VMEM((2, 128, 384), F32),
             pltpu.VMEM((H, 384), F32),
             pltpu.SMEM((2, 1), jnp.int32),
-            pltpu.VMEM((2, 128, D), F32),
+            pltpu.VMEM((2, H, 128, 384), BF16),
+            pltpu.VMEM((2, H, 128, 384), BF16),
             pltpu.VMEM((24, 1, 128), F32),
             pltpu.VMEM((24, 12, 1, 128), F32),
             pltpu.VMEM((32, 12, 1, 128), F32),
@@ -418,6 +505,8 @@
             dma((4,)),
             dma((2,)),
             dma((2,)),
+            dma((3,)),
+            dma((3,)),
             dma((H, 2)),
             dma((H, 2)),
             dma((H, 2)),
@@ -425,9 +514,9 @@
             dma((H, 2)),
             dma((H, 2)),
             dma(()),
-            dma((2,)),
+            dma((3,)),
             dma(()),
-            dma((2,)),
+            dma((3,)),
             dma(()),
             dma(()),
             dma((3,)),

time: 49.7 us -> 45.2 us (0.909)
  Pallas kernels: 47.6 us -> 43.1 us
    pallas_call x1, Pallas kernels: 46.6 us -> 42.1 us  [on_device(): pl.pallas_call(main_kernel, out_shape=(jax.ShapeDtypeStruct((2, 2, BLOCK,...]
where the time goes in v3:
time: 45.2 us; the launch traced here: 45 us
  Pallas kernels  43.1 us (95%)
  between operations  1.93 us (4%)
    pallas_call x1, Pallas kernels, on_device(): pl.pallas_call(main_kernel, out_shape=(jax.ShapeDtypeStruct((2, 2, BLOCK,...  42.1 us
    pallas_call x1, Pallas kernels, on_device(): pl.pallas_call(copy_kernel, out_shape=(whole, whole, whole, whole, jax.Sh...  1.01 us

profile of v3, /device:TPU:1, one launch (start us, length us, event | category | flops | bytes accessed | tf_op | source)
XLA Modules:
  0.0 45.0 jit_solution(5268989483143801483)
XLA Ops:
  1.9 42.1 %attention.1 = (bf16[2,2,128,1024]{3,2,1,0:T(8,128)(2,1)S(1)}, f32[8,384]{1,0:T(8,128)S(1)}) custom-call(bf16[1,128,1024]{2,1,0:T(8,128)(2,1)} %q_ref.1, bf16[1,128,1024]{2,1,0:T(8,128)(2,1)} %k_ref.1, bf16[1,128,1024]{2,1,0:T(8,128)(2,1)} %v_ref.1, bf16[1,128,1024]{2,1,0:T(8,128)(2,1)} %g_ref.1, s32[1,1]{1,0:T(1,128)S(6)} %copy.12.pos_ref, ...), custom_call_target="tpu_custom_call" | custom-call | tf_op jit(solution)/shard_map/attention/pallas_call | solution.py:483
  44.0 1.0 %results.1 = (bf16[1,128,1024]{2,1,0:T(8,128)(2,1)}, bf16[1,128,1024]{2,1,0:T(8,128)(2,1)}, bf16[1,128,1024]{2,1,0:T(8,128)(2,1)}, bf16[1,128,1024]{2,1,0:T(8,128)(2,1)}, f32[8,384]{1,0:T(8,128)}) custom-call(bf16[2,2,128,1024]{3,2,1,0:T(8,128)(2,1)S(1)} %get-tuple-element.7.res_ref, f32[8,384]{1,0:T(8,128)S(1)} %get-tuple-element.8.bg_ref), custom_call_target="tpu_custom_call" | custom-call | tf_op jit(solution)/shard_map/results/pallas_call | solution.py:530

commit v4 on v3

--- a/solution.py
+++ b/solution.py
@@ -70,8 +70,8 @@
 def main_kernel(
     q_ref, k_ref, v_ref, g_ref, pos_ref, len_ref, bias_ref,
     res_ref, bg_ref,
-    wide, sibling, sibling_mask, toep, mask, bias, place, wts, slp, bl, r1, r2, fin,
-    load_sem, chip_send, chip_recv, extra_send, extra_recv, w1_send, w1_recv, rel_send, rel_recv, w2_send, w2_recv,
+    wide, sibling, sibling_mask, mixed_out, mixed_in, toep, mask, bias, place, wts, slp, bl, r1, r2, fin,
+    load_sem, chip_send, chip_recv, extra_send, extra_recv, mask_send, mask_recv, mix_send, mix_recv, w1_send, w1_recv, rel_send, rel_recv, w2_send, w2_recv,
     up_send, up_recv, flat_send, flat_recv, down_send, down_recv, small_sem,
 ):
     s = lax.axis_index("seq")
@@ -87,6 +87,23 @@
     ahead = {"seq": (s + 4 * c - 2 + n_seq) % n_seq, "grp": grp}
     behind = {"seq": (s + 2 - 4 * c + n_seq) % n_seq, "grp": grp}
 
+    barrier = pltpu.get_barrier_semaphore()
+
+    def greet(device):
+        pl.semaphore_signal(barrier, inc=1, device_id=device, device_id_type=MESH)
+
+    def line_peer(j):
+        return {"seq": s - m + j, "grp": grp}
+
+    def plane_peer(j):
+        t = (x * n_grp + grp + j) % 32
+        return {"seq": (t // n_grp) * 24 + m, "grp": t % n_grp}
+
+    adds = m < 2
+    greet(ahead)
+    greet(behind)
+    greet(sib)
+
     loads = []
     for i, (ref, side, part) in enumerate(
         ((q_ref, 1, 0), (g_ref, 1, 1), (k_ref, 0, 0), (v_ref, 0, 1))
@@ -105,23 +122,6 @@
         copy = pltpu.make_async_copy(src, dst, small_sem.at[i])
         copy.start()
         smalls.append(copy)
-    barrier = pltpu.get_barrier_semaphore()
-
-    def greet(device):
-        pl.semaphore_signal(barrier, inc=1, device_id=device, device_id_type=MESH)
-
-    def line_peer(j):
-        return {"seq": s - m + j, "grp": grp}
-
-    def plane_peer(j):
-        t = (x * n_grp + grp + j) % 32
-        return {"seq": (t // n_grp) * 24 + m, "grp": t % n_grp}
-
-    adds = m < 2
-    greet(ahead)
-    greet(behind)
-    greet(sib)
-
     @pl.when(adds)
     def _():
         for j in range(1, 32):
@@ -164,38 +164,50 @@
             device_id=sib, device_id_type=MESH,
         )
 
-    def chip_copy(part):
-        return pltpu.make_async_remote_copy(
-            src_ref=wide.at[e, part, pl.ds(own_row(e), 128)],
-            dst_ref=wide.at[e, part, pl.ds(128, 128)],
-            send_sem=chip_send.at[part], recv_sem=chip_recv.at[part],
+    def chip_copy(part, rest):
+        cols = pl.ds(pl.multiple_of(256 * (1 - c), 128), 768) if rest else pl.ds(pl.multiple_of(768 * c, 128), 256)
+        return pltpu.make_async_remote_copy(
+            src_ref=wide.at[e, part, pl.ds(own_row(e), 128), cols],
+            dst_ref=wide.at[e, part, pl.ds(128, 128), cols],
+            send_sem=chip_send.at[part, rest], recv_sem=chip_recv.at[part, rest],
             device_id=sib, device_id_type=MESH,
         )
 
-    for h in range(H):
+    def extra_copy(part):
+        return pltpu.make_async_remote_copy(
+            src_ref=wide.at[d, part, pl.ds(own_row(d), 128)], dst_ref=sibling.at[part],
+            send_sem=extra_send.at[part], recv_sem=extra_recv.at[part],
+            device_id=sib, device_id_type=MESH,
+        )
+
+    def mixed_copy(part):
+        return pltpu.make_async_remote_copy(
+            src_ref=mixed_out.at[part], dst_ref=mixed_in.at[part],
+            send_sem=mix_send.at[part], recv_sem=mix_recv.at[part],
+            device_id=ahead, device_id_type=MESH,
+        )
+
+    def mask_copy(core):
+        if core == 0:
+            src, dst = mask.at[0, :, pl.ds(0, 256)], sibling_mask
+        else:
+            src, dst = mask.at[1, pl.ds(0, 8), pl.ds(128, 256)], sibling_mask.at[pl.ds(0, 8)]
+        return pltpu.make_async_remote_copy(
+            src_ref=src, dst_ref=dst, send_sem=mask_send, recv_sem=mask_recv,
+            device_id=sib, device_id_type=MESH,
+        )
+
+    lead = 6 - 6 * c
+    lack = 6 * c
+    for part in range(2):
+        chip_copy(part, 0).start()
+    for h in (lead, lead + 1):
         first_copy(h, 0).start()
         first_copy(h, 1).start()
-    chip_copy(0).start()
-    chip_copy(1).start()
-
-    def extra_copy(part):
-        return pltpu.make_async_remote_copy(
-            src_ref=wide.at[0, part, pl.ds(256, 128)], dst_ref=sibling.at[part],
-            send_sem=extra_send.at[part], recv_sem=extra_recv.at[part],
-            device_id=sib, device_id_type=MESH,
-        )
-
-    def extra_mask():
-        return pltpu.make_async_remote_copy(
-            src_ref=mask.at[1, pl.ds(0, 8), pl.ds(128, 128)], dst_ref=sibling_mask,
-            send_sem=extra_send.at[2], recv_sem=extra_recv.at[2],
-            device_id=sib, device_id_type=MESH,
-        )
-
-    @pl.when(c == 1)
-    def _():
-        extra_copy(0).start()
-        extra_copy(1).start()
+    for part in range(2):
+        chip_copy(part, 1).start()
+    for part in range(2):
+        extra_copy(part).start()
 
     for copy in smalls:
         copy.wait()
@@ -209,6 +221,26 @@
     used = (lane < n - p * 128) & (lane >= row)
     mask[1] = jnp.where(used, inverse, 0.0)
 
+    for part in range(2):
+        chip_copy(part, 0).wait_recv()
+    use_sibling = jnp.where(p == 1, 1, 0) * jnp.where(n > 256, 1, 0)
+    for part in range(2):
+        theirs = wide[d, part, pl.ds(128, 128), pl.ds(pl.multiple_of(128 * lead, 128), 256)]
+        mine = wide[d, part, pl.ds(own_row(d), 128), pl.ds(256, 256)]
+        mixed_out[part] = jnp.where(use_sibling == 1, theirs, mine)
+        mixed_copy(part).start()
+    for h in (4, 5):
+        first_copy(h, 0).start()
+        first_copy(h, 1).start()
+
+    @pl.when(c == 0)
+    def _():
+        mask_copy(0).start()
+
+    @pl.when(c == 1)
+    def _():
+        mask_copy(1).start()
+
     def make_toep(side):
         def body(h, carry):
             b = jnp.broadcast_to(bias[pl.ds(h, 1), :] * 0.5, (8, 384))
@@ -223,29 +255,35 @@
 
         lax.fori_loop(0, H, body, 0, unroll=2)
 
-    @pl.when(c == 1)
-    def _():
-        extra_mask().start()
 
     make_toep(d)
     make_toep(e)
 
-    def scores(side, h, lo, width):
+    def entries(x, y, x3, y3, near, mk):
+        z = nt(x, x3) * (0.5 * SCALE) + near
+        pulled = nt(y, y3)
+        t = jnp.tanh(z)
+        w0 = z * t + z
+        sg = 0.5 * t + 0.5
+        return w0 * mk, pulled * (sg + w0 * (1.0 - sg)) * mk
+
+    def scores(side, h, lo, width, moved=None):
         cols = head_cols(h)
         rows = pl.ds(lo, width)
         other = 1 - side
         own = pl.ds(own_row(other), 128)
-        y = nt(wide[other, 0, own, cols], wide[side, 0, rows, cols])
-        y = y * (0.5 * SCALE) + toep[side, h, :, rows]
-        pulled = nt(wide[other, 1, own, cols], wide[side, 1, rows, cols])
-        t = jnp.tanh(y)
-        w0 = y * t + y
-        sg = 0.5 * t + 0.5
-        mk = mask[side, :, rows]
-        slopes = pulled * (sg + w0 * (1.0 - sg)) * mk
-        wts[side, h, :, rows] = (w0 * mk).astype(BF16)
+        x3, y3 = (wide[side, 0, rows, cols], wide[side, 1, rows, cols]) if moved is None else moved
+        weights, slopes = entries(
+            wide[other, 0, own, cols], wide[other, 1, own, cols], x3, y3,
+            toep[side, h, :, rows], mask[side, :, rows],
+        )
+        wts[side, h, :, rows] = weights.astype(BF16)
         slp[side, h, :, rows] = slopes.astype(BF16)
         return slopes
+
+    def sibling_scores(side, h, lo, x3, y3, mk):
+        cols = head_cols(h)
+        return entries(sibling[0, :, cols], sibling[1, :, cols], x3, y3, toep[side, h, :, lo : lo + 128], mk)[1]
 
     def outputs(side, h):
         cols = head_cols(h)
@@ -254,78 +292,106 @@
         res_ref[side, 0, :, cols] = o1.astype(BF16)
         res_ref[side, 1, :, cols] = (o2 * SCALE).astype(BF16)
 
-    def near_row(side):
-        return pl.multiple_of(128 * (1 - side), 128)
-
     first_core = c == 0
+    at = (0, 3, 6, 9, 18, 21, 12, 15)
+
+    def count(h, offset, slopes, turned):
+        f0, f1 = diagonals(slopes, 128, 1 if turned else 0)
+        low, high = (flip(f0), flip(f1)) if turned else (f1, f0)
+        k = at[h] + offset - 1
+        bl[k] = bl[k] + row_sum(low)
+        bl[k + 1] = bl[k + 1] + row_sum(high)
+
+    for part in range(2):
+        chip_copy(part, 1).wait_recv()
 
     def direct_near(h):
-        slopes = scores(d, h, near_row(d), 256)
+        slopes = scores(d, h, pl.multiple_of(128 * (1 - d), 128), 256)
         lanes = lax.broadcasted_iota(jnp.int32, (128, 256), 1)
         slopes = jnp.where(first_core | (lanes >= 128), slopes, 0.0)
         n0, n1, _ = diagonals(slopes, 256, c)
-        bl[3 * h] = row_sum(jnp.where(first_core, n0, flip(n0)))
-        bl[3 * h + 1] = row_sum(n1)
-
-    def first_far(h):
+        bl[at[h]] = row_sum(jnp.where(first_core, n0, flip(n0)))
+        bl[at[h] + 1] = row_sum(jnp.where(first_core, n1, 0.0))
+        bl[at[h] + 2] = jnp.zeros((1, 128), F32)
+
+    for h in range(H):
+        direct_near(h)
+
+    for part in range(2):
+        extra_copy(part).wait_recv()
+
+    @pl.when(c == 0)
+    def _():
+        mask_copy(1).wait_recv()
+
+    @pl.when(c == 1)
+    def _():
+        mask_copy(0).wait_recv()
+
+    def relay(h):
+        for part in range(2):
+            first_copy(h, part).wait_recv()
+            relay_copy(h, part).start()
+
+    def far_pairs(h, turned, siblings):
         cols = head_cols(h)
-        f0, f1 = diagonals(scores(1, h, 256, 128), 128, 0)
-        y = nt(sibling[0, :, cols], wide[1, 0, 256:, cols]) * (0.5 * SCALE) + toep[1, h, :, 128:256]
-        pulled = nt(sibling[1, :, cols], wide[1, 1, 256:, cols])
-        t = jnp.tanh(y)
-        w0 = y * t + y
-        sg = 0.5 * t + 0.5
-        slopes = pulled * (sg + w0 * (1.0 - sg)) * sibling_mask[0:1, :]
-        g0, g1 = diagonals(slopes, 128, 0)
-        bl[3 * h] = bl[3 * h] + row_sum(g1)
-        bl[3 * h + 1] = bl[3 * h + 1] + row_sum(f1 + g0)
-        bl[3 * h + 2] = row_sum(f0)
-
-    def second_far(h):
-        f0, f1 = diagonals(scores(0, h, 0, 128), 128, 1)
-        bl[3 * h + 1] = row_sum(flip(f0))
-        bl[3 * h + 2] = row_sum(flip(f1))
-
-    chip_copy(0).wait_recv()
-    chip_copy(1).wait_recv()
-
-    def start_near(i, carry):
-        for h in range(4):
-            direct_near(4 * i + h)
-        return carry
-
-    lax.fori_loop(0, 2, start_near, 0)
-
-    @pl.when(c == 0)
-    def _():
-        for part in range(2):
-            extra_copy(part).wait_recv()
-        extra_mask().wait_recv()
-
-    def arrive(group):
-        heads = (2 * group, 2 * group + 1)
-        for h in heads:
-            for part in range(2):
-                first_copy(h, part).wait_recv()
-                relay_copy(h, part).start()
-
+        if turned:
+            count(h, 2, scores(0, h, 0, 128), True)
+            if siblings:
+                mk = sibling_mask[:, 128:]
+                count(h, 1, sibling_scores(0, h, 128, wide[0, 0, :128, cols], wide[0, 1, :128, cols], mk), True)
+        else:
+            count(h, 2, scores(1, h, 256, 128), False)
+            mk = sibling_mask[0:1, :128]
+            count(h, 1, sibling_scores(1, h, 128, wide[1, 0, 256:, cols], wide[1, 1, 256:, cols], mk), False)
+
+    def mixed_pairs(turned):
+        for i in range(2):
+            moved = tuple(mixed_in[part, :, 128 * i : 128 * i + 128] for part in range(2))
+            if turned:
+                count(2 + i, 2, scores(0, 2 + i, 0, 128, moved), True)
+                third = sibling_mask[:, :128]
+                count(i, 2, sibling_scores(0, i, 0, *moved, third), True)
+                second = jnp.where(third > 0.0, 0.0, sibling_mask[:, 128:])
+                count(2 + i, 1, sibling_scores(0, 2 + i, 128, *moved, second), True)
+            else:
+                count(2 + i, 2, scores(1, 2 + i, 256, 128, moved), False)
+                second = jnp.where(mask[1, 0:1, 256:] > 0.0, sibling_mask[0:1, :128], 0.0)
+                count(2 + i, 1, sibling_scores(1, 2 + i, 128, *moved, second), False)
+                third = sibling_mask[0:1, 128:]
+                count(6 + i, 2, sibling_scores(1, 6 + i, 256, *moved, third), False)
+
+    def both(todo):
         @pl.when(c == 0)
         def _():
-            for h in heads:
-                first_far(h)
+            todo(False)
 
         @pl.when(c == 1)
         def _():
-            for h in heads:
-                second_far(h)
+            todo(True)
+
+    def arrive_lead(turned):
+        for h in (0, 1) if turned else (6, 7):
+            relay(h)
+        for h in (0, 1) if turned else (6, 7):
+            far_pairs(h, turned, True)
+
+    def arrive_one(h):
+        relay(h)
+        both(lambda turned: far_pairs(h, turned, False))
+
+    def arrive_mixed():
+        for part in range(2):
+            mixed_copy(part).wait_recv()
+        both(mixed_pairs)
 
     me = x * n_grp + grp
     order = [8 * i + j for j in (0, 1, 2, 3, 7, 6, 4, 5) for i in (0, 2, 3, 1)]
 
     def rows_of(group, half):
-        return pl.ds(6 * half, 6) if group == 0 else pl.ds(6 + 6 * group + 3 * half, 3)
-
-    part_of = (pl.ds(0, 6), pl.ds(6, 3), pl.ds(9, 3))
+        return pl.ds(9 * half, 9) if group == 0 else pl.ds(18 + 3 * half, 3)
+
+    part_of = (pl.ds(0, 9), pl.ds(9, 3))
 
     def up_copy(group, half):
         return pltpu.make_async_remote_copy(
@@ -385,56 +451,68 @@
         for j in range(2, 24):
             down_copy(group, j).start()
 
-    arrive(0)
-    arrive(1)
+    both(arrive_lead)
+    arrive_mixed()
     send_up(0)
-    arrive(2)
+    arrive_one(4)
+    arrive_one(5)
     send_up(1)
-    arrive(3)
-    send_up(2)
-
-    def start_second(h, carry):
+
+    for h in (lead, lead + 1, 4, 5):
         for part in range(2):
             first_copy(h, part).wait_send()
+    for part in range(2):
+        mixed_copy(part).wait_send()
+    for h in (lack, lack + 1, 2, 3):
+        for part in range(2):
+            first_copy(h, part).start()
+    for h in range(H):
+        for part in range(2):
             second_copy(h, part).start()
+
+    def early(i, carry):
+        h = jnp.where(i < 2, lead + i, 2 + i)
+        outputs(d, h)
         return carry
 
-    lax.fori_loop(0, H, start_second, 0)
-
-    def rest(i, carry):
-        for h in range(2):
-            outputs(d, 2 * i + h)
+    lax.fori_loop(0, 4, early, 0, unroll=2)
+
+    @pl.when(adds)
+    def _():
+        for group in range(2):
+            add_line(group)
+
+    for h in (lack, lack + 1, 2, 3):
+        relay(h)
+    for h in (lack, lack + 1):
+        scores(d, h, far_row(d), 128)
+    for h in (lack, lack + 1, 2, 3):
+        outputs(d, h)
+
+    def finish(i, carry):
+        for h in (2 * i, 2 * i + 1):
             for part in range(2):
-                relay_copy(2 * i + h, part).wait_recv()
-            scores(e, 2 * i + h, near_row(e), 256)
+                relay_copy(h, part).wait_recv()
+                second_copy(h, part).wait_recv()
+        for h in (2 * i, 2 * i + 1):
+            scores(e, h, 0, 384)
+        for h in (2 * i, 2 * i + 1):
+            outputs(e, h)
         return carry
 
-    lax.fori_loop(0, H // 2, rest, 0)
-
-    @pl.when(adds)
-    def _():
-        for group in range(3):
-            add_line(group)
-
-    def finish(i, carry):
-        for h in range(2):
-            for part in range(2):
-                second_copy(2 * i + h, part).wait_recv()
-        for h in range(2):
-            scores(e, 2 * i + h, far_row(e), 128)
-        for h in range(2):
-            outputs(e, 2 * i + h)
-        return carry
-
     lax.fori_loop(0, H // 2, finish, 0)
     for part in range(2):
-        chip_copy(part).wait_send()
+        for rest in range(2):
+            chip_copy(part, rest).wait_send()
+        extra_copy(part).wait_send()
+
+    @pl.when(c == 0)
+    def _():
+        mask_copy(0).wait_send()
 
     @pl.when(c == 1)
     def _():
-        for part in range(2):
-            extra_copy(part).wait_send()
-        extra_mask().wait_send()
+        mask_copy(1).wait_send()
 
     def drain(h, carry):
         for part in range(2):
@@ -443,10 +521,13 @@
         return carry
 
     lax.fori_loop(0, H, drain, 0)
+    for h in (lack, lack + 1, 2, 3):
+        for part in range(2):
+            first_copy(h, part).wait_send()
 
     @pl.when(adds)
     def _():
-        for group in range(3):
+        for group in range(2):
             add_plane(group)
         bytes_of(r1.at[0], up_send, down_recv).wait()
         bytes_of(r2.at[pl.ds(0, 31)], flat_send, down_recv).wait_send()
@@ -458,7 +539,7 @@
 
     for h in range(H):
         for k in range(3):
-            bg_ref[h : h + 1, 128 * k : 128 * k + 128] = fin[3 * h + k]
+            bg_ref[h : h + 1, 128 * k : 128 * k + 128] = fin[at[h] + k]
 
 
 def copy_kernel(res_ref, bg_ref, att_ref, qg_ref, kg_ref, vg_ref, bias_ref, sem):
@@ -491,7 +572,9 @@
         scratch_shapes=[
             pltpu.VMEM((2, 2, 384, D), BF16),
             pltpu.VMEM((2, 128, D), BF16),
-            pltpu.VMEM((8, 128), F32),
+            pltpu.VMEM((128, 256), F32),
+            pltpu.VMEM((2, 128, 256), BF16),
+            pltpu.VMEM((2, 128, 256), BF16),
             pltpu.VMEM((2, H, 128, 384), F32),
             pltpu.VMEM((2, 128, 384), F32),
             pltpu.VMEM((H, 384), F32),
@@ -503,10 +586,14 @@
             pltpu.VMEM((32, 12, 1, 128), F32),
             pltpu.VMEM((24, 1, 128), F32),
             dma((4,)),
+            dma((2, 2)),
+            dma((2, 2)),
             dma((2,)),
             dma((2,)),
-            dma((3,)),
-            dma((3,)),
+            dma(()),
+            dma(()),
+            dma((2,)),
+            dma((2,)),
             dma((H, 2)),
             dma((H, 2)),
             dma((H, 2)),

time: 45.2 us -> 44.4 us (0.982)
  Pallas kernels: 43.1 us -> 42.3 us
    pallas_call x1, Pallas kernels: 42.1 us -> 41.3 us  [on_device(): pl.pallas_call(main_kernel, out_shape=(jax.ShapeDtypeStruct((2, 2, BLOCK,...]
where the time goes in v4:
time: 44.4 us; the launch traced here: 44.2 us
  Pallas kernels  42.3 us (95%)
  between operations  1.93 us (4%)
    pallas_call x1, Pallas kernels, on_device(): pl.pallas_call(main_kernel, out_shape=(jax.ShapeDtypeStruct((2, 2, BLOCK,...  41.3 us
    pallas_call x1, Pallas kernels, on_device(): pl.pallas_call(copy_kernel, out_shape=(whole, whole, whole, whole, jax.Sh...  1.01 us

profile of v4, /device:TPU:1, one launch (start us, length us, event | category | flops | bytes accessed | tf_op | source)
XLA Modules:
  0.0 44.2 jit_solution(16375160508709740176)
XLA Ops:
  1.9 41.3 %attention.1 = (bf16[2,2,128,1024]{3,2,1,0:T(8,128)(2,1)S(1)}, f32[8,384]{1,0:T(8,128)S(1)}) custom-call(bf16[1,128,1024]{2,1,0:T(8,128)(2,1)} %q_ref.1, bf16[1,128,1024]{2,1,0:T(8,128)(2,1)} %k_ref.1, bf16[1,128,1024]{2,1,0:T(8,128)(2,1)} %v_ref.1, bf16[1,128,1024]{2,1,0:T(8,128)(2,1)} %g_ref.1, s32[1,1]{1,0:T(1,128)S(6)} %copy.12.pos_ref, ...), custom_call_target="tpu_custom_call" | custom-call | tf_op jit(solution)/shard_map/attention/pallas_call | solution.py:564
  43.2 1.0 %results.1 = (bf16[1,128,1024]{2,1,0:T(8,128)(2,1)}, bf16[1,128,1024]{2,1,0:T(8,128)(2,1)}, bf16[1,128,1024]{2,1,0:T(8,128)(2,1)}, bf16[1,128,1024]{2,1,0:T(8,128)(2,1)}, f32[8,384]{1,0:T(8,128)}) custom-call(bf16[2,2,128,1024]{3,2,1,0:T(8,128)(2,1)S(1)} %get-tuple-element.7.res_ref, f32[8,384]{1,0:T(8,128)S(1)} %get-tuple-element.8.bg_ref), custom_call_target="tpu_custom_call" | custom-call | tf_op jit(solution)/shard_map/results/pallas_call | solution.py:617

commit v5 on v4

--- a/solution.py
+++ b/solution.py
@@ -99,7 +99,7 @@
         t = (x * n_grp + grp + j) % 32
         return {"seq": (t // n_grp) * 24 + m, "grp": t % n_grp}
 
-    adds = m < 2
+    adds = m == 1
     greet(ahead)
     greet(behind)
     greet(sib)
@@ -136,9 +136,13 @@
     def _():
         pl.semaphore_wait(barrier, 3 + 31)
 
-    @pl.when(jnp.logical_not(adds))
-    def _():
-        pl.semaphore_wait(barrier, 3 + 2)
+    @pl.when(m == 0)
+    def _():
+        pl.semaphore_wait(barrier, 3)
+
+    @pl.when(m > 1)
+    def _():
+        pl.semaphore_wait(barrier, 3 + 1)
 
     def piece(side, part, rows, h):
         return wide.at[side, part, pl.ds(rows, 128), head_cols(h)]
@@ -150,10 +154,21 @@
             device_id=ahead, device_id_type=MESH,
         )
 
-    def second_copy(h, part):
-        return pltpu.make_async_remote_copy(
-            src_ref=piece(e, part, own_row(e), h), dst_ref=piece(e, part, far_row(e), h),
-            send_sem=w2_send.at[h, part], recv_sem=w2_recv.at[h, part],
+    def pair_copy(h, part):
+        cols = pl.ds(pl.multiple_of(h * 128, 128), 256)
+        return pltpu.make_async_remote_copy(
+            src_ref=wide.at[d, part, pl.ds(own_row(d), 128), cols],
+            dst_ref=wide.at[d, part, pl.ds(far_row(d), 128), cols],
+            send_sem=w1_send.at[h, part], recv_sem=w1_recv.at[h, part],
+            device_id=ahead, device_id_type=MESH,
+        )
+
+    def second_copy(i, part):
+        cols = pl.ds(512 * i, 512)
+        return pltpu.make_async_remote_copy(
+            src_ref=wide.at[e, part, pl.ds(own_row(e), 128), cols],
+            dst_ref=wide.at[e, part, pl.ds(far_row(e), 128), cols],
+            send_sem=w2_send.at[i, part], recv_sem=w2_recv.at[i, part],
             device_id=behind, device_id_type=MESH,
         )
 
@@ -257,7 +272,6 @@
 
 
     make_toep(d)
-    make_toep(e)
 
     def entries(x, y, x3, y3, near, mk):
         z = nt(x, x3) * (0.5 * SCALE) + near
@@ -387,29 +401,28 @@
 
     me = x * n_grp + grp
     order = [8 * i + j for j in (0, 1, 2, 3, 7, 6, 4, 5) for i in (0, 2, 3, 1)]
-
-    def rows_of(group, half):
-        return pl.ds(9 * half, 9) if group == 0 else pl.ds(18 + 3 * half, 3)
-
-    part_of = (pl.ds(0, 9), pl.ds(9, 3))
-
-    def up_copy(group, half):
-        return pltpu.make_async_remote_copy(
-            src_ref=bl.at[rows_of(group, half)], dst_ref=r1.at[m, part_of[group]],
+    part_of = (pl.ds(0, 18), pl.ds(18, 6))
+
+    def up_copy(group):
+        part = part_of[group]
+        return pltpu.make_async_remote_copy(
+            src_ref=bl.at[part], dst_ref=r1.at[m, part],
             send_sem=up_send, recv_sem=up_recv.at[group],
-            device_id=line_peer(half), device_id_type=MESH,
+            device_id=line_peer(1), device_id_type=MESH,
         )
 
     def flat_copy(group, j):
-        return pltpu.make_async_remote_copy(
-            src_ref=r2.at[me, part_of[group]], dst_ref=r2.at[me, part_of[group]],
+        part = part_of[group]
+        return pltpu.make_async_remote_copy(
+            src_ref=r2.at[me, part], dst_ref=r2.at[me, part],
             send_sem=flat_send, recv_sem=flat_recv.at[group],
             device_id={"seq": (j // 8) * 24 + m, "grp": j % 8}, device_id_type=MESH,
         )
 
     def down_copy(group, j):
-        return pltpu.make_async_remote_copy(
-            src_ref=fin.at[rows_of(group, c)], dst_ref=fin.at[rows_of(group, c)],
+        part = part_of[group]
+        return pltpu.make_async_remote_copy(
+            src_ref=fin.at[part], dst_ref=fin.at[part],
             send_sem=down_send, recv_sem=down_recv,
             device_id=line_peer(j), device_id_type=MESH,
         )
@@ -423,18 +436,15 @@
     def send_up(group):
         @pl.when(adds)
         def _():
-            up_copy(group, 1 - c).start()
-            r1[m, part_of[group]] = bl[rows_of(group, c)]
+            r1[m, part_of[group]] = bl[part_of[group]]
 
         @pl.when(jnp.logical_not(adds))
         def _():
-            up_copy(group, 0).start()
-            up_copy(group, 1).start()
+            up_copy(group).start()
 
     def add_line(group):
         part = part_of[group]
-        others = r1.at[pl.ds(0, 23), part]
-        bytes_of(others, up_send, up_recv.at[group]).wait_recv()
+        bytes_of(r1.at[pl.ds(0, 23), part], up_send, up_recv.at[group]).wait_recv()
         r2[me, part] = jnp.sum(r1[:, part], axis=0)
         for j in order:
 
@@ -444,31 +454,32 @@
 
     def add_plane(group):
         part = part_of[group]
-        others = r2.at[pl.ds(0, 31), part]
-        bytes_of(others, flat_send, flat_recv.at[group]).wait_recv()
-        fin[rows_of(group, c)] = jnp.sum(r2[:, part], axis=0) * (n_seq * n_grp) ** (-0.5)
-        down_copy(group, 1 - c).start()
-        for j in range(2, 24):
+        bytes_of(r2.at[pl.ds(0, 31), part], flat_send, flat_recv.at[group]).wait_recv()
+        fin[part] = jnp.sum(r2[:, part], axis=0) * (n_seq * n_grp) ** (-0.5)
+        for j in (0, *range(2, 6)):
             down_copy(group, j).start()
+
+        @pl.when((me > 0) | (group == 0))
+        def _():
+            for j in range(6, 24):
+                down_copy(group, j).start()
 
     both(arrive_lead)
     arrive_mixed()
     send_up(0)
     arrive_one(4)
+
     arrive_one(5)
     send_up(1)
 
-    for h in (lead, lead + 1, 4, 5):
+    for h in (lack, 2):
         for part in range(2):
-            first_copy(h, part).wait_send()
-    for part in range(2):
-        mixed_copy(part).wait_send()
-    for h in (lack, lack + 1, 2, 3):
+            pair_copy(h, part).start()
+    for i in range(2):
         for part in range(2):
-            first_copy(h, part).start()
-    for h in range(H):
-        for part in range(2):
-            second_copy(h, part).start()
+            second_copy(i, part).start()
+
+    make_toep(e)
 
     def early(i, carry):
         h = jnp.where(i < 2, lead + i, 2 + i)
@@ -482,25 +493,26 @@
         for group in range(2):
             add_line(group)
 
-    for h in (lack, lack + 1, 2, 3):
-        relay(h)
+    for h in (lack, 2):
+        for part in range(2):
+            pair_copy(h, part).wait_recv()
+            relay_copy(h, part).start()
+            relay_copy(h + 1, part).start()
     for h in (lack, lack + 1):
         scores(d, h, far_row(d), 128)
     for h in (lack, lack + 1, 2, 3):
         outputs(d, h)
 
-    def finish(i, carry):
-        for h in (2 * i, 2 * i + 1):
-            for part in range(2):
+    for i in range(2):
+        heads = range(4 * i, 4 * i + 4)
+        for part in range(2):
+            for h in heads:
                 relay_copy(h, part).wait_recv()
-                second_copy(h, part).wait_recv()
-        for h in (2 * i, 2 * i + 1):
+            second_copy(i, part).wait_recv()
+        for h in heads:
             scores(e, h, 0, 384)
-        for h in (2 * i, 2 * i + 1):
+        for h in heads:
             outputs(e, h)
-        return carry
-
-    lax.fori_loop(0, H // 2, finish, 0)
     for part in range(2):
         for rest in range(2):
             chip_copy(part, rest).wait_send()
@@ -517,25 +529,39 @@
     def drain(h, carry):
         for part in range(2):
             relay_copy(h, part).wait_send()
-            second_copy(h, part).wait_send()
         return carry
 
     lax.fori_loop(0, H, drain, 0)
-    for h in (lack, lack + 1, 2, 3):
-        for part in range(2):
+    for part in range(2):
+        for h in (lead, lead + 1, 4, 5):
             first_copy(h, part).wait_send()
+        mixed_copy(part).wait_send()
+        for h in (lack, 2):
+            pair_copy(h, part).wait_send()
+        for i in range(2):
+            second_copy(i, part).wait_send()
 
     @pl.when(adds)
     def _():
         for group in range(2):
             add_plane(group)
-        bytes_of(r1.at[0], up_send, down_recv).wait()
         bytes_of(r2.at[pl.ds(0, 31)], flat_send, down_recv).wait_send()
-        bytes_of(r1.at[pl.ds(0, 23)], down_send, down_recv).wait_send()
+        bytes_of(r1.at[pl.ds(0, 23), part_of[0]], down_send, down_recv).wait_send()
+        bytes_of(r1.at[pl.ds(0, 5), part_of[1]], down_send, down_recv).wait_send()
+
+        @pl.when(me > 0)
+        def _():
+            bytes_of(r1.at[pl.ds(0, 18), part_of[1]], down_send, down_recv).wait_send()
 
     @pl.when(jnp.logical_not(adds))
     def _():
         bytes_of(fin, up_send, down_recv).wait()
+
+    @pl.when((m == 0) & (me == 0))
+    def _():
+        for j in range(6, 24):
+            down_copy(1, j).start()
+        bytes_of(r1.at[pl.ds(0, 18), part_of[1]], down_send, down_recv).wait_send()
 
     for h in range(H):
         for k in range(3):
@@ -582,8 +608,8 @@
             pltpu.VMEM((2, H, 128, 384), BF16),
             pltpu.VMEM((2, H, 128, 384), BF16),
             pltpu.VMEM((24, 1, 128), F32),
-            pltpu.VMEM((24, 12, 1, 128), F32),
-            pltpu.VMEM((32, 12, 1, 128), F32),
+            pltpu.VMEM((24, 24, 1, 128), F32),
+            pltpu.VMEM((32, 24, 1, 128), F32),
             pltpu.VMEM((24, 1, 128), F32),
             dma((4,)),
             dma((2, 2)),

time: 44.4 us -> 43.4 us (0.977)
  Pallas kernels: 42.3 us -> 41.3 us
    pallas_call x1, Pallas kernels: 41.3 us -> 40.3 us  [on_device(): pl.pallas_call(main_kernel, out_shape=(jax.ShapeDtypeStruct((2, 2, BLOCK,...]
where the time goes in v5:
time: 43.4 us; the launch traced here: 43.2 us
  Pallas kernels  41.3 us (95%)
  between operations  1.93 us (4%)
    pallas_call x1, Pallas kernels, on_device(): pl.pallas_call(main_kernel, out_shape=(jax.ShapeDtypeStruct((2, 2, BLOCK,...  40.3 us
    pallas_call x1, Pallas kernels, on_device(): pl.pallas_call(copy_kernel, out_shape=(whole, whole, whole, whole, jax.Sh...  1.01 us

profile of v5, /device:TPU:1, one launch (start us, length us, event | category | flops | bytes accessed | tf_op | source)
XLA Modules:
  0.0 43.2 jit_solution(15769880680059754963)
XLA Ops:
  1.9 40.3 %attention.1 = (bf16[2,2,128,1024]{3,2,1,0:T(8,128)(2,1)S(1)}, f32[8,384]{1,0:T(8,128)S(1)}) custom-call(bf16[1,128,1024]{2,1,0:T(8,128)(2,1)} %q_ref.1, bf16[1,128,1024]{2,1,0:T(8,128)(2,1)} %k_ref.1, bf16[1,128,1024]{2,1,0:T(8,128)(2,1)} %v_ref.1, bf16[1,128,1024]{2,1,0:T(8,128)(2,1)} %g_ref.1, s32[1,1]{1,0:T(1,128)S(6)} %copy.12.pos_ref, ...), custom_call_target="tpu_custom_call" | custom-call | tf_op jit(solution)/shard_map/attention/pallas_call | solution.py:590
  42.2 1.0 %results.1 = (bf16[1,128,1024]{2,1,0:T(8,128)(2,1)}, bf16[1,128,1024]{2,1,0:T(8,128)(2,1)}, bf16[1,128,1024]{2,1,0:T(8,128)(2,1)}, bf16[1,128,1024]{2,1,0:T(8,128)(2,1)}, f32[8,384]{1,0:T(8,128)}) custom-call(bf16[2,2,128,1024]{3,2,1,0:T(8,128)(2,1)S(1)} %get-tuple-element.7.res_ref, f32[8,384]{1,0:T(8,128)S(1)} %get-tuple-element.8.bg_ref), custom_call_target="tpu_custom_call" | custom-call | tf_op jit(solution)/shard_map/results/pallas_call | solution.py:643

commit v6 on v5

--- a/solution.py
+++ b/solution.py
@@ -446,7 +446,7 @@
         part = part_of[group]
         bytes_of(r1.at[pl.ds(0, 23), part], up_send, up_recv.at[group]).wait_recv()
         r2[me, part] = jnp.sum(r1[:, part], axis=0)
-        for j in order:
+        for j in order[:8]:
 
             @pl.when(me != j)
             def _(j=j):
@@ -492,6 +492,12 @@
     def _():
         for group in range(2):
             add_line(group)
+        for j in order[8:]:
+
+            @pl.when(me != j)
+            def _(j=j):
+                flat_copy(0, j).start()
+                flat_copy(1, j).start()
 
     for h in (lack, 2):
         for part in range(2):

time: 43.4 us -> 43 us (level)
  no operation moved by 1% of the time
where the time goes in v6:
time: 43 us; the launch traced here: 42.8 us
  Pallas kernels  40.9 us (95%)
  between operations  1.93 us (4%)
    pallas_call x1, Pallas kernels, on_device(): pl.pallas_call(main_kernel, out_shape=(jax.ShapeDtypeStruct((2, 2, BLOCK,...  39.9 us
    pallas_call x1, Pallas kernels, on_device(): pl.pallas_call(copy_kernel, out_shape=(whole, whole, whole, whole, jax.Sh...  1.01 us

profile of v6, /device:TPU:1, one launch (start us, length us, event | category | flops | bytes accessed | tf_op | source)
XLA Modules:
  0.0 42.8 jit_solution(15455410659103759664)
XLA Ops:
  1.9 39.9 %attention.1 = (bf16[2,2,128,1024]{3,2,1,0:T(8,128)(2,1)S(1)}, f32[8,384]{1,0:T(8,128)S(1)}) custom-call(bf16[1,128,1024]{2,1,0:T(8,128)(2,1)} %q_ref.1, bf16[1,128,1024]{2,1,0:T(8,128)(2,1)} %k_ref.1, bf16[1,128,1024]{2,1,0:T(8,128)(2,1)} %v_ref.1, bf16[1,128,1024]{2,1,0:T(8,128)(2,1)} %g_ref.1, s32[1,1]{1,0:T(1,128)S(6)} %copy.12.pos_ref, ...), custom_call_target="tpu_custom_call" | custom-call | tf_op jit(solution)/shard_map/attention/pallas_call | solution.py:596
  41.8 1.0 %results.1 = (bf16[1,128,1024]{2,1,0:T(8,128)(2,1)}, bf16[1,128,1024]{2,1,0:T(8,128)(2,1)}, bf16[1,128,1024]{2,1,0:T(8,128)(2,1)}, bf16[1,128,1024]{2,1,0:T(8,128)(2,1)}, f32[8,384]{1,0:T(8,128)}) custom-call(bf16[2,2,128,1024]{3,2,1,0:T(8,128)(2,1)S(1)} %get-tuple-element.7.res_ref, f32[8,384]{1,0:T(8,128)S(1)} %get-tuple-element.8.bg_ref), custom_call_target="tpu_custom_call" | custom-call | tf_op jit(solution)/shard_map/results/pallas_call | solution.py:649
